TPU v7x, 128 devices: a whole 4x4x4 slice. The times are simulated.
128 devices in a mesh: seg: 8 (over z, y_lo), slab: 16 (over x, y_hi, core).
Axes of the slice: x: 4, y: 4 (y_hi: 2, y_lo: 2; y = y_hi * 2 + y_lo), z: 4, core: 2. Of those that a mesh axis runs over, the one named last changes fastest.
Arguments:
- state: float32 [8, 2, 4, 64, 64, 128], P('seg', None, None, 'slab'), may hold values from -6 to 6
- base_flow: float32 [8, 3, 64, 64, 128], P('seg', None, 'slab'), may hold values from -0.6 to 1.7, as said below
Outputs:
- advanced: float32 [8, 2, 4, 64, 64, 128], P('seg', None, None, 'slab')
- residual: float32 [8, 2, 4, 64, 64, 128], P('seg', None, None, 'slab')
Inputs may be any that keep to these rules, and one draw needn't show every extreme that they name: `base_flow`: component 0 of the base flow lies between 1.3 and 1.7 in every cell; components 1 and 2 lie between -0.6 and 1.4.
All inputs are finite; a program needn't handle non-finite values.
Results may differ from a plain program's by a relative error of at most 0.00002.
Values sent between devices are 32-bit elements; how exact they have to be, the bound alone decides.
No kernel may reach another device: no remote copies, remote signals or barrier semaphores. Data moves between devices by JAX's collectives and lax.ppermute only.
A program may use at most 128 MiB of HBM per device.

v0:
```python
import functools

import jax
import jax.numpy as jnp
from jax import lax
from jax.experimental import pallas as pl
from jax.experimental.pallas import tpu as pltpu
from jax.sharding import PartitionSpec as P

time_step = 0.4
viscosity = 0.067
sound_sq = 1.0

OWN = 4
HALO = 2
WIDE = OWN + 2 * HALO
TILE = 8
F32 = jnp.float32


def core():
    return lax.rem(lax.axis_index("slab"), 2)


def at_end():
    slab = lax.axis_index("slab")
    return jnp.logical_or(slab == 0, slab == lax.axis_size("slab") - 1)


def outer_side(width):
    far = core() * (OWN - width)
    return far, (OWN - width) - far


def rows_around(ref, field, plane, row, rows):
    here = ref[field, plane, row : row + TILE, :]
    index = lax.broadcasted_iota(jnp.int32, here.shape, 0)
    if row == 0:
        below = jnp.where(index == 0, 0.0, pltpu.roll(here, 1, 0))
    else:
        below = ref[field, plane, row - 1 : row - 1 + TILE, :]
    if row + TILE == rows:
        above = jnp.where(index == TILE - 1, 0.0, pltpu.roll(here, TILE - 1, 0))
    else:
        above = ref[field, plane, row + 1 : row + 1 + TILE, :]
    return here, below, above


def around(ref, field, plane, row, rows):
    here, y_below, y_above = rows_around(ref, field, plane, row, rows)
    lanes = here.shape[1]
    return (
        here,
        ref[field, plane - 1, row : row + TILE, :],
        ref[field, plane + 1, row : row + TILE, :],
        y_below,
        y_above,
        pltpu.roll(here, 1, 1),
        pltpu.roll(here, lanes - 1, 1),
    )


def tile_rates(q, flow, plane, row, rows):
    fields = [around(q, j, plane, row, rows) for j in range(4)]
    base = [around(flow, j, plane, row, rows) for j in range(3)]
    press = fields[3]
    half = [0.5 * b[0] for b in base]
    lower = [viscosity + h for h in half]
    upper = [viscosity - h for h in half]
    react = [-0.5 * f[0] for f in fields[:3]]
    rates = []
    for j in range(3):
        f, b = fields[j], base[j]
        total = (-6.0 * viscosity) * f[0]
        for i in range(3):
            total = total + lower[i] * f[1 + 2 * i]
            total = total + upper[i] * f[2 + 2 * i]
            total = total + react[i] * (b[2 + 2 * i] - b[1 + 2 * i])
        total = total - 0.5 * (press[2 + 2 * j] - press[1 + 2 * j])
        rates.append(total)
    div = (fields[0][2] - fields[0][1]) + (fields[1][4] - fields[1][3])
    div = div + (fields[2][6] - fields[2][5])
    rates.append((-0.5 * sound_sq) * div)
    return [f[0] for f in fields], rates


def over_tiles(first, last, rows, body):
    @pl.loop(first, last)
    def _(plane):
        for row in range(0, rows, TILE):
            body(plane, row)


def run_copies(copies):
    for copy in copies:
        copy.start()
    for copy in copies:
        copy.wait()


def zero_planes(ref, first, width):
    ref[:, pl.ds(first, width)] = jnp.zeros((ref.shape[0], width) + ref.shape[2:], F32)


def pack_kernel(state, flow, far_a, near, sems):
    far, close = outer_side(HALO)
    pairs = [
        (flow.at[0, :, pl.ds(far, HALO)], far_a.at[0:3]),
        (state.at[0, 0, :, pl.ds(far, HALO)], far_a.at[3:7]),
        (flow.at[0, :, pl.ds(close, HALO)], near.at[0:3]),
        (state.at[0, 0, :, pl.ds(close, HALO)], near.at[3:7]),
        (state.at[0, 1, :, pl.ds(close, HALO)], near.at[7:11]),
    ]
    run_copies([pltpu.make_async_copy(a, b, sems.at[i]) for i, (a, b) in enumerate(pairs)])


def stage_one(q, base, second, first, count):
    rows = q.shape[2]

    def one(plane, row):
        here, rates = tile_rates(q, base, plane, row, rows)
        for j in range(4):
            second[j, plane, row : row + TILE, :] = here[j] + (time_step / 2) * rates[j]

    over_tiles(first, first + count, rows, one)


def stage_two(q, base, second, mid, part, first, count, shift):
    rows = q.shape[2]

    def two(plane, row):
        here, rates = tile_rates(second, base, plane, row, rows)
        for j in range(4):
            start = q[j, plane, row : row + TILE, :]
            third = start + (time_step / 2) * rates[j]
            mid[j, plane - shift, row : row + TILE, :] = third
            part[j, plane - shift, row : row + TILE, :] = (here[j] + 2.0 * third - start) * (1.0 / 3.0)

    over_tiles(first, first + count, rows, two)


def inner_kernel(vec, state, flow, near, after, second_out, mid, part, *rest):
    del after
    far_out = rest[0] if vec else None
    q, base, second, sems = rest[-4:]
    close = (1 - core()) * (OWN + HALO)
    pairs = [
        (state.at[0, vec], q.at[:, HALO : HALO + OWN]),
        (flow.at[0], base.at[:, HALO : HALO + OWN]),
        (near.at[0:3], base.at[:, pl.ds(close, HALO)]),
        (near.at[3 + 4 * vec : 7 + 4 * vec], q.at[:, pl.ds(close, HALO)]),
    ]
    run_copies([pltpu.make_async_copy(a, b, sems.at[i]) for i, (a, b) in enumerate(pairs)])
    lowest = 3 - 2 * core()
    stage_one(q, base, second, lowest, OWN)
    second_out[...] = second[:, pl.ds(lowest, OWN)]
    stage_two(q, base, second, mid, part, lowest + 1, HALO, lowest + 1)
    if vec:
        far, _ = outer_side(HALO)
        far_out[...] = q[:, pl.ds(HALO + far, HALO)]


def first_kernel(vec, far_at, state, flow, near, far_flow, far_q, second_in, mid_in, part_in, after, mid, part, far_out, q, base, second, sems):
    del after
    far, close = core() * (OWN + HALO), (1 - core()) * (OWN + HALO)
    outer, inner = HALO * core(), HALO * (1 - core())
    pairs = [
        (state.at[0, vec, :, pl.ds(outer, HALO)], q.at[:, pl.ds(HALO + outer, HALO)]),
        (flow.at[0], base.at[:, HALO : HALO + OWN]),
        (far_flow.at[0:3], base.at[:, pl.ds(far, HALO)]),
        (far_q.at[far_at : far_at + 4], q.at[:, pl.ds(far, HALO)]),
        (second_in, second.at[:, pl.ds(3 - 2 * core(), OWN)]),
        (mid_in, mid.at[:, pl.ds(inner, HALO)]),
        (part_in, part.at[:, pl.ds(inner, HALO)]),
    ]
    run_copies([pltpu.make_async_copy(a, b, sems.at[i]) for i, (a, b) in enumerate(pairs)])

    @pl.when(at_end())
    def _():
        zero_planes(q, far, HALO)
        zero_planes(base, far, HALO)

    stage_one(q, base, second, 1 + OWN * core(), HALO)

    @pl.when(at_end())
    def _():
        zero_planes(second, 1 + core() * (WIDE - 3), 1)

    stage_two(q, base, second, mid, part, HALO + outer, HALO, HALO)
    far, _ = outer_side(HALO)
    far_out[...] = mid[:, pl.ds(far, HALO)]


def second_kernel(vec, far_at, state, flow, near, far_flow, far_q, mid, part, far_mid, near_mid, after, out, q, base, third, fourth, held, sems):
    del after
    rows = q.shape[2]
    far, close = core() * (OWN + HALO), (1 - core()) * (OWN + HALO)
    pairs = [
        (state.at[0, vec], q.at[:, HALO : HALO + OWN]),
        (flow.at[0], base.at[:, HALO : HALO + OWN]),
        (near.at[0:3], base.at[:, pl.ds(close, HALO)]),
        (near.at[3 + 4 * vec : 7 + 4 * vec], q.at[:, pl.ds(close, HALO)]),
        (far_flow.at[0:3], base.at[:, pl.ds(far, HALO)]),
        (far_q.at[far_at : far_at + 4], q.at[:, pl.ds(far, HALO)]),
        (mid, third.at[:, HALO : HALO + OWN]),
        (near_mid, third.at[:, pl.ds(close, HALO)]),
        (far_mid, third.at[:, pl.ds(far, HALO)]),
        (part, held),
    ]
    run_copies([pltpu.make_async_copy(a, b, sems.at[i]) for i, (a, b) in enumerate(pairs)])

    @pl.when(at_end())
    def _():
        zero_planes(third, far, HALO)
        zero_planes(base, far, HALO)

    def one(plane, row):
        _, rates = tile_rates(third, base, plane, row, rows)
        for j in range(4):
            fourth[j, plane, row : row + TILE, :] = q[j, plane, row : row + TILE, :] + time_step * rates[j]

    over_tiles(1, WIDE - 1, rows, one)

    @pl.when(at_end())
    def _():
        zero_planes(fourth, 1 + core() * (WIDE - 3), 1)

    def two(plane, row):
        here, rates = tile_rates(fourth, base, plane, row, rows)
        for j in range(4):
            total = held[j, plane - HALO, row : row + TILE, :] + (1.0 / 3.0) * here[j]
            out[j, plane - HALO, row : row + TILE, :] = total + (time_step / 6) * rates[j]

    over_tiles(HALO, HALO + OWN, rows, two)


def shards(state, flow):
    rows, lanes = state.shape[-2:]
    slabs, segs = lax.axis_size("slab"), lax.axis_size("seg")
    near_pairs = [(i, i ^ 1) for i in range(slabs)]
    seg_pairs = [(i, (i + 1) % segs) for i in range(segs)]
    far_pairs = []
    for seg in range(segs):
        for slab in range(slabs):
            if slab in (0, slabs - 1):
                to = (seg ^ 2) * slabs + slab
            else:
                to = seg * slabs + (slab + 1 if slab % 2 else slab - 1)
            far_pairs.append((seg * slabs + slab, to))

    def far_swap(value):
        return lax.ppermute(value, ("seg", "slab"), far_pairs)

    def near_swap(value):
        return lax.ppermute(value, "slab", near_pairs)

    def planes(fields, count):
        return jax.ShapeDtypeStruct((fields, count, rows, lanes), F32)

    def scratch(fields, count):
        return pltpu.VMEM((fields, count, rows, lanes), F32)

    anywhere = pl.BlockSpec(memory_space=pl.ANY)
    vmem = pl.BlockSpec(memory_space=pltpu.VMEM)
    cost = pl.CostEstimate(flops=30_000_000, bytes_accessed=6_000_000, transcendentals=0)
    params = pltpu.CompilerParams(vmem_limit_bytes=16 * 1024 * 1024)

    far_a, near = pl.pallas_call(
        pack_kernel,
        out_shape=(pltpu.VMEM((7, HALO, rows, lanes), F32), pltpu.VMEM((11, HALO, rows, lanes), F32)),
        in_specs=[anywhere] * 2,
        out_specs=(vmem,) * 2,
        scratch_shapes=[pltpu.SemaphoreType.DMA((5,))],
        compiler_params=params,
        name="pack",
    )(pltpu.with_memory_space_constraint(state, pltpu.HBM), pltpu.with_memory_space_constraint(flow, pltpu.HBM))
    far_a = far_swap(far_a)
    near = near_swap(near)

    def inner(vec, after):
        return pl.pallas_call(
            functools.partial(inner_kernel, vec),
            out_shape=(planes(4, OWN), planes(4, HALO), planes(4, HALO)) + (planes(4, HALO),) * vec,
            in_specs=[anywhere] * 4,
            out_specs=(vmem,) * (3 + vec),
            scratch_shapes=[scratch(4, WIDE), scratch(3, WIDE), scratch(4, WIDE), pltpu.SemaphoreType.DMA((4,))],
            compiler_params=params,
            cost_estimate=cost,
            name=f"inner_{vec}",
        )(state, flow, near, after)

    inner0 = inner(0, near)
    *inner1, far_b = inner(1, inner0[1])
    far_b = far_swap(far_b)

    def first(vec, ready, after):
        far_at, far_q = (3, far_a) if vec == 0 else (0, far_b)
        return pl.pallas_call(
            functools.partial(first_kernel, vec, far_at),
            out_shape=(planes(4, OWN), planes(4, OWN), planes(4, HALO)),
            in_specs=[anywhere] * 9,
            out_specs=(vmem,) * 3,
            scratch_shapes=[scratch(4, WIDE), scratch(3, WIDE), scratch(4, WIDE), pltpu.SemaphoreType.DMA((7,))],
            compiler_params=params,
            cost_estimate=cost,
            name=f"first_{vec}",
        )(state, flow, near, far_a, far_q, *ready, after)

    def second(vec, mid, part, far_mid, near_mid, after):
        far_at, far_q = (3, far_a) if vec == 0 else (0, far_b)
        return pl.pallas_call(
            functools.partial(second_kernel, vec, far_at),
            out_shape=planes(4, OWN),
            in_specs=[anywhere] * 10,
            out_specs=vmem,
            scratch_shapes=[
                scratch(4, WIDE),
                scratch(3, WIDE),
                scratch(4, WIDE),
                scratch(4, WIDE),
                scratch(4, OWN),
                pltpu.SemaphoreType.DMA((10,)),
            ],
            compiler_params=params,
            cost_estimate=cost,
            name=f"second_{vec}",
        )(state, flow, near, far_a, far_q, mid, part, far_mid, near_mid, after)

    near0, near1 = near_swap(inner0[1]), near_swap(inner1[1])
    mid0, part0, far0 = first(0, inner0, inner1[1])
    far0 = far_swap(far0)
    mid1, part1, far1 = first(1, inner1, mid0)
    far1 = far_swap(far1)
    out0 = second(0, mid0, part0, far0, near0, mid1)
    prev0 = lax.ppermute(out0, "seg", seg_pairs)
    out1 = second(1, mid1, part1, far1, near1, out0)
    prev1 = lax.ppermute(out1, "seg", seg_pairs)
    advanced = jnp.stack([out0, out1])[None]
    residual = jnp.stack([state[0, 0] - prev0, state[0, 1] - prev1])[None]
    return advanced, residual


def solution(mesh):
    return jax.shard_map(
        shards,
        mesh=mesh,
        in_specs=(P("seg", None, None, "slab", None, None), P("seg", None, "slab", None, None)),
        out_specs=(
            P("seg", None, None, "slab", None, None),
            P("seg", None, None, "slab", None, None),
        ),
        check_vma=False,
    )
```

profile of v0, /device:TPU:1, one launch (start us, length us, event | category | flops | bytes accessed | tf_op | source)
XLA Modules:
  0.0 61.7 jit_solution(18131401867572705093)
XLA Ops:
  0.6 1.5 %pack.1 = (f32[7,2,64,128]{3,2,1,0:T(8,128)S(1)}, f32[11,2,64,128]{3,2,1,0:T(8,128)S(1)}) custom-call(f32[1,2,4,4,64,128]{5,4,3,2,1,0:T(8,128)} %state.13, f32[1,3,4,64,128]{4,3,2,1,0:T(8,128)} %flow.13), custom_call_target="tpu_custom_call" | custom-call | tf_op jit(solution)/shard_map/pack/pallas_call | solution.py:268
  2.1 1.5 %collective-permute-start = (f32[11,2,64,128]{3,2,1,0:T(8,128)S(1)}, f32[11,2,64,128]{3,2,1,0:T(8,128)S(1)}, u32[]{:S(2)}, u32[]{:S(2)}) collective-permute-start(f32[11,2,64,128]{3,2,1,0:T(8,128)S(1)} %get-tuple-element.17), channel_id=1, source_target_pairs={{0,1},{1,0},{2,3},{3,2},{4,5},{5,4},{6,7},{7,6},{8,9},{9,8},{10,11... | collective-permute-start | bytes 2162696 | tf_op jit(solution)/shard_map/ppermute | solution.py:255
  3.6 3.0 %collective-permute-start.1 = (f32[7,2,64,128]{3,2,1,0:T(8,128)S(1)}, f32[7,2,64,128]{3,2,1,0:T(8,128)S(1)}, u32[]{:S(2)}, u32[]{:S(2)}) collective-permute-start(f32[7,2,64,128]{3,2,1,0:T(8,128)S(1)} %get-tuple-element.18), channel_id=1, source_target_pairs={{0,32},{1,2},{2,1},{3,4},{4,3},{5,6},{6,5},{7,8},{8,7},{9,10},{10,... | collective-permute-start | bytes 1376264 | tf_op jit(solution)/shard_map/ppermute | solution.py:252
  6.6 1.4 %inner_0.1 = (f32[4,4,64,128]{3,2,1,0:T(8,128)S(1)}, f32[4,2,64,128]{3,2,1,0:T(8,128)S(1)}, f32[4,2,64,128]{3,2,1,0:T(8,128)S(1)}) custom-call(f32[1,2,4,4,64,128]{5,4,3,2,1,0:T(8,128)S(1)} %copy-done, f32[1,3,4,64,128]{4,3,2,1,0:T(8,128)S(1)} %copy-done.1, f32[11,2,64,128]{3,2,1,0:T(8,128)S(1)} %collective-permute-done.near.after, ...), custom_call_target="tpu_custom_call" | custom-call | flops 30000000 | bytes 6000000 | tf_op jit(solution)/shard_map/inner_0/pallas_call | solution.py:281
  8.1 1.5 %inner_1.1 = (f32[4,4,64,128]{3,2,1,0:T(8,128)S(1)}, f32[4,2,64,128]{3,2,1,0:T(8,128)S(1)}, f32[4,2,64,128]{3,2,1,0:T(8,128)S(1)}, f32[4,2,64,128]{3,2,1,0:T(8,128)S(1)}) custom-call(f32[1,2,4,4,64,128]{5,4,3,2,1,0:T(8,128)S(1)} %copy-done, f32[1,3,4,64,128]{4,3,2,1,0:T(8,128)S(1)} %copy-done.1, f32[11,2,64,128]{3,2,1,0:T(8,128)S(1)} %collective-permute-done.near.after, ...), custom_call_target="tpu_custom_call" | custom-call | flops 30000000 | bytes 6000000 | tf_op jit(solution)/shard_map/inner_1/pallas_call | solution.py:281
  9.5 2.2 %collective-permute-start.4 = (f32[4,2,64,128]{3,2,1,0:T(8,128)S(1)}, f32[4,2,64,128]{3,2,1,0:T(8,128)S(1)}, u32[]{:S(2)}, u32[]{:S(2)}) collective-permute-start(f32[4,2,64,128]{3,2,1,0:T(8,128)S(1)} %get-tuple-element.26), channel_id=1, source_target_pairs={{0,32},{1,2},{2,1},{3,4},{4,3},{5,6},{6,5},{7,8},{8,7},{9,10},{10,... | collective-permute-start | bytes 786440 | tf_op jit(solution)/shard_map/ppermute | solution.py:252
  11.7 0.5 collective-permute-start.6
  12.2 7.5 %collective-permute-done.1.far_flow.far_q = f32[7,2,64,128]{3,2,1,0:T(8,128)S(1)} collective-permute-done((f32[7,2,64,128]{3,2,1,0:T(8,128)S(1)}, f32[7,2,64,128]{3,2,1,0:T(8,128)S(1)}, u32[]{:S(2)}, u32[]{:S(2)}) %collective-permute-start.1) | collective-permute-done | bytes 458784 | tf_op jit(solution)/shard_map/ppermute | solution.py:252
  19.7 1.1 %first_0.1 = (f32[4,4,64,128]{3,2,1,0:T(8,128)S(1)}, f32[4,4,64,128]{3,2,1,0:T(8,128)S(1)}, f32[4,2,64,128]{3,2,1,0:T(8,128)S(1)}) custom-call(f32[1,2,4,4,64,128]{5,4,3,2,1,0:T(8,128)S(1)} %copy-done, f32[1,3,4,64,128]{4,3,2,1,0:T(8,128)S(1)} %copy-done.1, f32[11,2,64,128]{3,2,1,0:T(8,128)S(1)} %collective-permute-done.near.after, ...), custom_call_target="tpu_custom_call" | custom-call | flops 30000000 | bytes 6000000 | tf_op jit(solution)/shard_map/first_0/pallas_call | solution.py:298
  20.9 4.1 %collective-permute-start.2 = (f32[4,2,64,128]{3,2,1,0:T(8,128)S(1)}, f32[4,2,64,128]{3,2,1,0:T(8,128)S(1)}, u32[]{:S(2)}, u32[]{:S(2)}) collective-permute-start(f32[4,2,64,128]{3,2,1,0:T(8,128)S(1)} %get-tuple-element.25), channel_id=1, source_target_pairs={{0,32},{1,2},{2,1},{3,4},{4,3},{5,6},{6,5},{7,8},{8,7},{9,10},{10,... | collective-permute-start | bytes 786440 | tf_op jit(solution)/shard_map/ppermute | solution.py:252
  24.9 5.4 %collective-permute-done.4.far_q = f32[4,2,64,128]{3,2,1,0:T(8,128)S(1)} collective-permute-done((f32[4,2,64,128]{3,2,1,0:T(8,128)S(1)}, f32[4,2,64,128]{3,2,1,0:T(8,128)S(1)}, u32[]{:S(2)}, u32[]{:S(2)}) %collective-permute-start.4) | collective-permute-done | bytes 262176 | tf_op jit(solution)/shard_map/ppermute | solution.py:252
  30.3 1.1 %first_1.1 = (f32[4,4,64,128]{3,2,1,0:T(8,128)S(1)}, f32[4,4,64,128]{3,2,1,0:T(8,128)S(1)}, f32[4,2,64,128]{3,2,1,0:T(8,128)S(1)}) custom-call(f32[1,2,4,4,64,128]{5,4,3,2,1,0:T(8,128)S(1)} %copy-done, f32[1,3,4,64,128]{4,3,2,1,0:T(8,128)S(1)} %copy-done.1, f32[11,2,64,128]{3,2,1,0:T(8,128)S(1)} %collective-permute-done.near.after, ...), custom_call_target="tpu_custom_call" | custom-call | flops 30000000 | bytes 6000000 | tf_op jit(solution)/shard_map/first_1/pallas_call | solution.py:298
  31.5 4.1 %collective-permute-start.5 = (f32[4,2,64,128]{3,2,1,0:T(8,128)S(1)}, f32[4,2,64,128]{3,2,1,0:T(8,128)S(1)}, u32[]{:S(2)}, u32[]{:S(2)}) collective-permute-start(f32[4,2,64,128]{3,2,1,0:T(8,128)S(1)} %get-tuple-element.31), channel_id=1, source_target_pairs={{0,32},{1,2},{2,1},{3,4},{4,3},{5,6},{6,5},{7,8},{8,7},{9,10},{10,... | collective-permute-start | bytes 786440 | tf_op jit(solution)/shard_map/ppermute | solution.py:252
  35.5 0.4 collective-permute-done.2.far_mid
  35.9 2.4 %second_0.1.after = f32[4,4,64,128]{3,2,1,0:T(8,128)S(1)} custom-call(f32[1,2,4,4,64,128]{5,4,3,2,1,0:T(8,128)S(1)} %copy-done, f32[1,3,4,64,128]{4,3,2,1,0:T(8,128)S(1)} %copy-done.1, f32[11,2,64,128]{3,2,1,0:T(8,128)S(1)} %collective-permute-done.near.after, f32[7,2,64,128]{3,2,1,0:T(8,128)S(1)} %collective-permute-done.1.far_flow.far_q, ...), custom_call_target="tpu_custom_call" | custom-call | flops 30000000 | bytes 6000000 | tf_op jit(solution)/shard_map/second_0/pallas_call | solution.py:311
  38.4 0.3 collective-permute-start.7
  38.7 4.1 %collective-permute-done.5.far_mid = f32[4,2,64,128]{3,2,1,0:T(8,128)S(1)} collective-permute-done((f32[4,2,64,128]{3,2,1,0:T(8,128)S(1)}, f32[4,2,64,128]{3,2,1,0:T(8,128)S(1)}, u32[]{:S(2)}, u32[]{:S(2)}) %collective-permute-start.5) | collective-permute-done | bytes 262176 | tf_op jit(solution)/shard_map/ppermute | solution.py:252
  42.8 2.4 %second_1.1 = f32[4,4,64,128]{3,2,1,0:T(8,128)S(1)} custom-call(f32[1,2,4,4,64,128]{5,4,3,2,1,0:T(8,128)S(1)} %copy-done, f32[1,3,4,64,128]{4,3,2,1,0:T(8,128)S(1)} %copy-done.1, f32[11,2,64,128]{3,2,1,0:T(8,128)S(1)} %collective-permute-done.near.after, f32[7,2,64,128]{3,2,1,0:T(8,128)S(1)} %collective-permute-done.1.far_flow.far_q, ...), custom_call_target="tpu_custom_call" | custom-call | flops 30000000 | bytes 6000000 | tf_op jit(solution)/shard_map/second_1/pallas_call | solution.py:311
  45.2 0.1 collective-permute-start.8
  45.3 1.1 %maximum_bitcast_fusion = f32[1,2,4,4,64,128]{5,4,3,2,1,0:T(8,128)} fusion(f32[1,4,4,64,128]{4,3,2,1,0:T(8,128)S(1)} %bitcast.19, f32[1,4,4,64,128]{4,3,2,1,0:T(8,128)S(1)} %bitcast.18), kind=kLoop, calls=%fused_computation | loop fusion | flops 262144 | bytes 2097152 | tf_op jit(solution)/shard_map/broadcast_in_dim | solution.py:338
  46.4 8.6 %collective-permute-done.7 = f32[4,4,64,128]{3,2,1,0:T(8,128)S(1)} collective-permute-done((f32[4,4,64,128]{3,2,1,0:T(8,128)S(1)}, f32[4,4,64,128]{3,2,1,0:T(8,128)S(1)}, u32[]{:S(2)}, u32[]{:S(2)}) %collective-permute-start.7) | collective-permute-done | bytes 524320 | tf_op jit(solution)/shard_map/ppermute | solution.py:335
  54.9 5.6 %collective-permute-done.8 = f32[4,4,64,128]{3,2,1,0:T(8,128)S(1)} collective-permute-done((f32[4,4,64,128]{3,2,1,0:T(8,128)S(1)}, f32[4,4,64,128]{3,2,1,0:T(8,128)S(1)}, u32[]{:S(2)}, u32[]{:S(2)}) %collective-permute-start.8) | collective-permute-done | bytes 524320 | tf_op jit(solution)/shard_map/ppermute | solution.py:337
  60.6 0.1 fusion.1
  60.7 1.0 %maximum_bitcast_fusion.1 = f32[1,2,4,4,64,128]{5,4,3,2,1,0:T(8,128)} fusion(f32[1,4,4,64,128]{4,3,2,1,0:T(8,128)S(1)} %get-tuple-element.33, f32[1,4,4,64,128]{4,3,2,1,0:T(8,128)S(1)} %get-tuple-element.32), kind=kLoop, calls=%fused_computation.1 | loop fusion | flops 262144 | bytes 2097152 | tf_op jit(solution)/shard_map/broadcast_in_dim | solution.py:339
  (8 shorter events, 0.0 us)
Async XLA Ops:
  0.6 6.0 %copy-start = (f32[1,2,4,4,64,128]{5,4,3,2,1,0:T(8,128)S(1)}, f32[1,2,4,4,64,128]{5,4,3,2,1,0:T(8,128)}, u32[]{:S(2)}) copy-start(f32[1,2,4,4,64,128]{5,4,3,2,1,0:T(8,128)} %state.13) | copy-start | bytes 3145732
  0.6 6.0 %copy-start.1 = (f32[1,3,4,64,128]{4,3,2,1,0:T(8,128)S(1)}, f32[1,3,4,64,128]{4,3,2,1,0:T(8,128)}, u32[]{:S(2)}) copy-start(f32[1,3,4,64,128]{4,3,2,1,0:T(8,128)} %flow.13) | copy-start | bytes 1179652
  2.1 4.5 %collective-permute-start = (f32[11,2,64,128]{3,2,1,0:T(8,128)S(1)}, f32[11,2,64,128]{3,2,1,0:T(8,128)S(1)}, u32[]{:S(2)}, u32[]{:S(2)}) collective-permute-start(f32[11,2,64,128]{3,2,1,0:T(8,128)S(1)} %get-tuple-element.17), channel_id=1, source_target_pairs={{0,1},{1,0},{2,3},{3,2},{4,5},{5,4},{6,7},{7,6},{8,9},{9,8},{10,11... | collective-permute-start | bytes 2162696 | tf_op jit(solution)/shard_map/ppermute | solution.py:255
  3.6 16.1 %collective-permute-start.1 = (f32[7,2,64,128]{3,2,1,0:T(8,128)S(1)}, f32[7,2,64,128]{3,2,1,0:T(8,128)S(1)}, u32[]{:S(2)}, u32[]{:S(2)}) collective-permute-start(f32[7,2,64,128]{3,2,1,0:T(8,128)S(1)} %get-tuple-element.18), channel_id=1, source_target_pairs={{0,32},{1,2},{2,1},{3,4},{4,3},{5,6},{6,5},{7,8},{8,7},{9,10},{10,... | collective-permute-start | bytes 1376264 | tf_op jit(solution)/shard_map/ppermute | solution.py:252
  9.5 20.8 %collective-permute-start.4 = (f32[4,2,64,128]{3,2,1,0:T(8,128)S(1)}, f32[4,2,64,128]{3,2,1,0:T(8,128)S(1)}, u32[]{:S(2)}, u32[]{:S(2)}) collective-permute-start(f32[4,2,64,128]{3,2,1,0:T(8,128)S(1)} %get-tuple-element.26), channel_id=1, source_target_pairs={{0,32},{1,2},{2,1},{3,4},{4,3},{5,6},{6,5},{7,8},{8,7},{9,10},{10,... | collective-permute-start | bytes 786440 | tf_op jit(solution)/shard_map/ppermute | solution.py:252
  11.7 24.3 %collective-permute-start.3 = (f32[4,2,64,128]{3,2,1,0:T(8,128)S(1)}, f32[4,2,64,128]{3,2,1,0:T(8,128)S(1)}, u32[]{:S(2)}, u32[]{:S(2)}) collective-permute-start(f32[4,2,64,128]{3,2,1,0:T(8,128)S(1)} %get-tuple-element.20.after.mid_in), channel_id=1, source_target_pairs={{0,1},{1,0},{2,3},{3,2},{4,5},{5,4},{6,7},{7,6},{8,9},{9,8},{10,11... | collective-permute-start | bytes 786440 | tf_op jit(solution)/shard_map/ppermute | solution.py:255
  11.7 27.0 %collective-permute-start.6 = (f32[4,2,64,128]{3,2,1,0:T(8,128)S(1)}, f32[4,2,64,128]{3,2,1,0:T(8,128)S(1)}, u32[]{:S(2)}, u32[]{:S(2)}) collective-permute-start(f32[4,2,64,128]{3,2,1,0:T(8,128)S(1)} %get-tuple-element.22.after.mid_in), channel_id=1, source_target_pairs={{0,1},{1,0},{2,3},{3,2},{4,5},{5,4},{6,7},{7,6},{8,9},{9,8},{10,11... | collective-permute-start | bytes 786440 | tf_op jit(solution)/shard_map/ppermute | solution.py:255
  20.9 15.1 %collective-permute-start.2 = (f32[4,2,64,128]{3,2,1,0:T(8,128)S(1)}, f32[4,2,64,128]{3,2,1,0:T(8,128)S(1)}, u32[]{:S(2)}, u32[]{:S(2)}) collective-permute-start(f32[4,2,64,128]{3,2,1,0:T(8,128)S(1)} %get-tuple-element.25), channel_id=1, source_target_pairs={{0,32},{1,2},{2,1},{3,4},{4,3},{5,6},{6,5},{7,8},{8,7},{9,10},{10,... | collective-permute-start | bytes 786440 | tf_op jit(solution)/shard_map/ppermute | solution.py:252
  31.5 11.3 %collective-permute-start.5 = (f32[4,2,64,128]{3,2,1,0:T(8,128)S(1)}, f32[4,2,64,128]{3,2,1,0:T(8,128)S(1)}, u32[]{:S(2)}, u32[]{:S(2)}) collective-permute-start(f32[4,2,64,128]{3,2,1,0:T(8,128)S(1)} %get-tuple-element.31), channel_id=1, source_target_pairs={{0,32},{1,2},{2,1},{3,4},{4,3},{5,6},{6,5},{7,8},{8,7},{9,10},{10,... | collective-permute-start | bytes 786440 | tf_op jit(solution)/shard_map/ppermute | solution.py:252
  38.4 16.5 %collective-permute-start.7 = (f32[4,4,64,128]{3,2,1,0:T(8,128)S(1)}, f32[4,4,64,128]{3,2,1,0:T(8,128)S(1)}, u32[]{:S(2)}, u32[]{:S(2)}) collective-permute-start(f32[4,4,64,128]{3,2,1,0:T(8,128)S(1)} %second_0.1.after), channel_id=1, source_target_pairs={{0,16},{16,32},{32,48},{48,64},{64,80},{80,96},{96,112},{112,0},{1... | collective-permute-start | bytes 1572872 | tf_op jit(solution)/shard_map/ppermute | solution.py:335
  45.2 15.4 %collective-permute-start.8 = (f32[4,4,64,128]{3,2,1,0:T(8,128)S(1)}, f32[4,4,64,128]{3,2,1,0:T(8,128)S(1)}, u32[]{:S(2)}, u32[]{:S(2)}) collective-permute-start(f32[4,4,64,128]{3,2,1,0:T(8,128)S(1)} %second_1.1), channel_id=1, source_target_pairs={{0,16},{16,32},{32,48},{48,64},{64,80},{80,96},{96,112},{112,0},{1... | collective-permute-start | bytes 1572872 | tf_op jit(solution)/shard_map/ppermute | solution.py:337
where the time goes:
time: 61.9 us; the launch traced here: 61.7 us
  waiting for transfers between devices  31.6 us (51%)
  starting transfers between devices  15.6 us (25%)
  Pallas kernels  11.5 us (19%)
  other arithmetic  2.26 us (4%)
  between operations  0.72 us (1%)
    ppermute x4, waiting for transfers between devices, far_swap(): return lax.ppermute(value, ('seg', 'slab'), far_pairs)  17.4 us
    ppermute x4, starting transfers between devices, far_swap(): return lax.ppermute(value, ('seg', 'slab'), far_pairs)  13.3 us
    ppermute x1, waiting for transfers between devices, shards(): prev0 = lax.ppermute(out0, 'seg', seg_pairs)  8.58 us
    ppermute x1, waiting for transfers between devices, shards(): prev1 = lax.ppermute(out1, 'seg', seg_pairs)  5.62 us
    pallas_call x2, Pallas kernels, second(): pl.pallas_call(functools.partial(second_kernel, vec, far_at), out_shape=p...  4.88 us
    pallas_call x2, Pallas kernels, inner(): pl.pallas_call(functools.partial(inner_kernel, vec), out_shape=(planes(4,...  2.91 us
    pallas_call x2, Pallas kernels, first(): pl.pallas_call(functools.partial(first_kernel, vec, far_at), out_shape=(p...  2.26 us
    ppermute x3, starting transfers between devices, near_swap(): return lax.ppermute(value, 'slab', near_pairs)  2.01 us
  transfers between devices with their start and end apart: 9, of which 6 were waited for; matrix products, arithmetic and copies ran while one was open for 2% of the time, Pallas kernels for 16%

commit v1 on v0

v1 whole, which is shorter than its diff:
```python
import functools

import jax
import jax.numpy as jnp
from jax import lax
from jax.experimental import pallas as pl
from jax.experimental.pallas import tpu as pltpu
from jax.sharding import PartitionSpec as P

time_step = 0.4
viscosity = 0.067
sound_sq = 1.0

OWN = 4
HALO = 2
WIDE = OWN + 2 * HALO
TILE = 8
COEFS = 12
COEF_PLANES = OWN + 1
F32 = jnp.float32


def core():
    return lax.rem(lax.axis_index("slab"), 2)


def at_end():
    slab = lax.axis_index("slab")
    return jnp.logical_or(slab == 0, slab == lax.axis_size("slab") - 1)


def far_edge():
    return HALO + (OWN - 1) * core()


def far_beyond():
    return HALO - 1 + (OWN + 1) * core()


def near_halo():
    return (1 - core()) * (OWN + HALO)


def coef_first():
    return HALO - core()


def far_sign():
    return 1.0 - 2.0 * core().astype(F32)


def tile_of(ref, field, plane, row):
    return ref[field, plane, row : row + TILE, :]


def around(ref, field, plane, row, rows):
    here = tile_of(ref, field, plane, row)
    index = lax.broadcasted_iota(jnp.int32, here.shape, 0)
    if row == 0:
        y_below = jnp.where(index == 0, 0.0, pltpu.roll(here, 1, 0))
    else:
        y_below = ref[field, plane, row - 1 : row - 1 + TILE, :]
    if row + TILE == rows:
        y_above = jnp.where(index == TILE - 1, 0.0, pltpu.roll(here, TILE - 1, 0))
    else:
        y_above = ref[field, plane, row + 1 : row + 1 + TILE, :]
    lanes = here.shape[1]
    return (
        here,
        tile_of(ref, field, plane - 1, row),
        tile_of(ref, field, plane + 1, row),
        y_below,
        y_above,
        pltpu.roll(here, 1, 1),
        pltpu.roll(here, lanes - 1, 1),
    )


def tile_coefs(base, plane, coefs, place, row, rows):
    for j in range(3):
        b = around(base, j, plane, row, rows)
        coefs[j, place, row : row + TILE, :] = 0.5 * b[0]
        for i in range(3):
            coefs[3 + 3 * i + j, place, row : row + TILE, :] = 0.5 * (b[1 + 2 * i] - b[2 + 2 * i])


def tile_rates(q, coefs, plane, place, row, rows, beyond=None):
    fields = [around(q, j, plane, row, rows) for j in range(4)]
    press = fields[3]
    half = [tile_of(coefs, i, place, row) for i in range(3)]
    lower = [viscosity + h for h in half]
    upper = [viscosity - h for h in half]
    rates = []
    for j in range(3):
        f = fields[j]
        total = (-6.0 * viscosity) * f[0] - 0.5 * (press[2 + 2 * j] - press[1 + 2 * j])
        for i in range(3):
            total = total + lower[i] * f[1 + 2 * i]
            total = total + upper[i] * f[2 + 2 * i]
            total = total + fields[i][0] * tile_of(coefs, 3 + 3 * i + j, place, row)
        if beyond is not None:
            total = total + fields[0][0] * tile_of(beyond, j, 0, row)
        rates.append(total)
    div = (fields[0][2] - fields[0][1]) + (fields[1][4] - fields[1][3])
    div = div + (fields[2][6] - fields[2][5])
    rates.append((-0.5 * sound_sq) * div)
    return [f[0] for f in fields], rates


def over_tiles(first, count, rows, body):
    @pl.loop(first, first + count)
    def _(plane):
        for row in range(0, rows, TILE):
            body(plane, row)


def over_rates(q, coefs, first, count, store, beyond=None):
    rows = q.shape[2]

    def body(plane, row):
        here, rates = tile_rates(q, coefs, plane, plane - coef_first(), row, rows, beyond)
        store(here, rates, plane, row)

    over_tiles(first, count, rows, body)


def partial_rates(q, coefs, plane, place, out, first):
    rows = q.shape[2]
    for row in range(0, rows, TILE):
        _, rates = tile_rates(q, coefs, plane, place, row, rows)
        for j in range(4):
            out[first + j, 0, row : row + TILE, :] = rates[j]


def finish_halo(q, partial, coefs, beyond, store):
    sign, plane, edge = far_sign(), far_beyond(), far_edge()
    place = edge - coef_first()
    for row in range(0, q.shape[2], TILE):
        here = [tile_of(q, j, plane, row) for j in range(4)]
        own = [tile_of(q, j, edge, row) for j in range(4)]
        factor = viscosity - tile_of(beyond, 0, 0, row)
        scaled = sign * here[0]
        rates = [
            tile_of(partial, j, 0, row) + factor * own[j] - scaled * tile_of(coefs, j, place, row)
            for j in range(3)
        ]
        rates[0] = rates[0] - (0.5 * sign) * own[3]
        rates.append(tile_of(partial, 3, 0, row) - (0.5 * sound_sq * sign) * own[0])
        store(here, rates, plane, row)


def start_copies(pairs, sems):
    copies = [pltpu.make_async_copy(a, b, sems.at[i]) for i, (a, b) in enumerate(pairs)]
    for copy in copies:
        copy.start()
    return copies


def run_copies(pairs, sems):
    for copy in start_copies(pairs, sems):
        copy.wait()


def zero_planes(ref, first, width):
    ref[:, pl.ds(first, width)] = jnp.zeros((ref.shape[0], width) + ref.shape[2:], F32)


def read_beyond(flow, ref):
    sign = jnp.where(at_end(), 0.0, 0.5 * far_sign())
    ref[...] = sign * flow[...]


def pack_kernel(state, flow, far_a, near, q, base, coefs, sems):
    far, close, edge = core() * (OWN - HALO), (1 - core()) * (OWN - HALO), core() * (OWN - 1)
    pairs = [
        (flow.at[0, :, pl.ds(far, HALO)], base.at[:, pl.ds(1 - core(), HALO)]),
        (state.at[0, 0, :, pl.ds(far, HALO)], q.at[:, pl.ds(1 - core(), HALO)]),
        (flow.at[0, :, pl.ds(edge, 1)], far_a.at[0:3]),
        (state.at[0, 0, :, pl.ds(edge, 1)], far_a.at[3:7]),
        (flow.at[0, :, pl.ds(close, HALO)], near.at[0:3]),
        (state.at[0, 0, :, pl.ds(close, HALO)], near.at[3:7]),
        (state.at[0, 1, :, pl.ds(close, HALO)], near.at[7:11]),
    ]
    copies = start_copies(pairs, sems)
    zero_planes(q, 2 * core(), 1)
    zero_planes(base, 2 * core(), 1)
    copies[0].wait()
    rows = q.shape[2]
    for row in range(0, rows, TILE):
        tile_coefs(base, 1, coefs, 0, row, rows)
    copies[1].wait()
    partial_rates(q, coefs, 1, 0, far_a, 7)
    for copy in copies[2:]:
        copy.wait()


def inner_stages(q, coefs, second, second_out, mid, part):
    lowest = 3 - 2 * core()

    def one(here, rates, plane, row):
        for j in range(4):
            value = here[j] + (time_step / 2) * rates[j]
            second[j, plane, row : row + TILE, :] = value
            second_out[j, plane - lowest, row : row + TILE, :] = value

    over_rates(q, coefs, lowest, OWN, one)
    over_rates(second, coefs, lowest + 1, HALO, second_stage(q, mid, part, lowest + 1))


def second_stage(q, mid, part, shift):
    def two(here, rates, plane, row):
        for j in range(4):
            start = tile_of(q, j, plane, row)
            third = start + (time_step / 2) * rates[j]
            mid[j, plane - shift, row : row + TILE, :] = third
            part[j, plane - shift, row : row + TILE, :] = (here[j] + 2.0 * third - start) * (1.0 / 3.0)

    return two


def inner_0_kernel(state, flow, near, coefs, own0, own1, second_out, mid, part, q, base, second, sems):
    pairs = [
        (flow.at[0], base.at[:, HALO : HALO + OWN]),
        (near.at[0:3], base.at[:, pl.ds(near_halo(), HALO)]),
        (state.at[0, 0], q.at[:, HALO : HALO + OWN]),
        (near.at[3:7], q.at[:, pl.ds(near_halo(), HALO)]),
        (state.at[0, 0], own0),
        (state.at[0, 1], own1),
    ]
    copies = start_copies(pairs, sems)
    zero_planes(base, far_beyond(), 1)
    for copy in copies[:2]:
        copy.wait()
    rows = q.shape[2]
    over_tiles(
        coef_first(),
        COEF_PLANES,
        rows,
        lambda plane, row: tile_coefs(base, plane, coefs, plane - coef_first(), row, rows),
    )
    for copy in copies[2:]:
        copy.wait()
    inner_stages(q, coefs, second, second_out, mid, part)


def inner_1_kernel(own, near, coefs, mid_other, second_out, mid, part, far_out, near_out, q, second, sems):
    pairs = [
        (own, q.at[:, HALO : HALO + OWN]),
        (near.at[7:11], q.at[:, pl.ds(near_halo(), HALO)]),
        (mid_other, near_out.at[0:4]),
    ]
    run_copies(pairs, sems)
    zero_planes(q, far_beyond(), 1)
    far_out[0:4] = q[:, pl.ds(far_edge(), 1)]
    partial_rates(q, coefs, far_edge(), far_edge() - coef_first(), far_out, 4)
    inner_stages(q, coefs, second, second_out, mid, part)
    near_out[4:8] = mid[...]


def first_kernel(far_at, own, coefs, far_a, far_q, second_in, mid_in, part_in, after, also_after, mid, part, far_out, q, second, third, partial, beyond, raw, sems):
    del after, also_after
    outer, inner = HALO * core(), HALO * (1 - core())
    edge, halo = far_edge(), far_beyond()
    pairs = [
        (own.at[:, pl.ds(outer, HALO)], q.at[:, pl.ds(HALO + outer, HALO)]),
        (far_a.at[0:3], raw),
        (far_q.at[far_at : far_at + 4], q.at[:, pl.ds(halo, 1)]),
        (far_q.at[far_at + 4 : far_at + 8], partial),
        (second_in, second.at[:, pl.ds(3 - 2 * core(), OWN)]),
        (mid_in, mid.at[:, pl.ds(inner, HALO)]),
        (part_in, part.at[:, pl.ds(inner, HALO)]),
    ]
    run_copies(pairs, sems)
    read_beyond(raw, beyond)

    @pl.when(at_end())
    def _():
        zero_planes(q, halo, 1)

    def one(here, rates, plane, row):
        for j in range(4):
            second[j, plane, row : row + TILE, :] = here[j] + (time_step / 2) * rates[j]

    finish_halo(q, partial, coefs, beyond, one)

    @pl.when(at_end())
    def _():
        zero_planes(second, halo, 1)

    over_rates(q, coefs, edge, 1, one, beyond)
    two = second_stage(q, mid, part, HALO)
    over_rates(second, coefs, edge, 1, two, beyond)
    over_rates(second, coefs, edge + 1 - 2 * core(), 1, two)
    third[:, pl.ds(HALO + outer, HALO)] = mid[:, pl.ds(outer, HALO)]
    zero_planes(third, halo, 1)
    far_out[0:4] = third[:, pl.ds(edge, 1)]
    partial_rates(third, coefs, edge, edge - coef_first(), far_out, 4)


def second_kernel(near_at, far_at, own, coefs, near, far_a, far_q, mid, part, far_mid, near_mid, after, out, q, third, fourth, partial, beyond, raw, sems):
    del after
    edge, halo, close = far_edge(), far_beyond(), near_halo()
    mid_at = near_at - 3
    pairs = [
        (own, q.at[:, HALO : HALO + OWN]),
        (near.at[near_at : near_at + 4], q.at[:, pl.ds(close, HALO)]),
        (far_a.at[0:3], raw),
        (far_q.at[far_at : far_at + 4], q.at[:, pl.ds(halo, 1)]),
        (mid, third.at[:, HALO : HALO + OWN]),
        (near_mid.at[mid_at : mid_at + 4], third.at[:, pl.ds(close, HALO)]),
        (far_mid.at[0:4], third.at[:, pl.ds(halo, 1)]),
        (far_mid.at[4:8], partial),
    ]
    run_copies(pairs, sems)
    read_beyond(raw, beyond)

    @pl.when(at_end())
    def _():
        zero_planes(third, halo, 1)

    def one(here, rates, plane, row):
        for j in range(4):
            fourth[j, plane, row : row + TILE, :] = tile_of(q, j, plane, row) + time_step * rates[j]

    finish_halo(third, partial, coefs, beyond, one)

    @pl.when(at_end())
    def _():
        zero_planes(fourth, halo, 1)

    over_rates(third, coefs, edge, 1, one, beyond)
    over_rates(third, coefs, 3 - 2 * core(), OWN, one)

    def two(here, rates, plane, row):
        for j in range(4):
            total = tile_of(part, j, plane - HALO, row) + (1.0 / 3.0) * here[j]
            out[j, plane - HALO, row : row + TILE, :] = total + (time_step / 6) * rates[j]

    over_rates(fourth, coefs, edge, 1, two, beyond)
    over_rates(fourth, coefs, 3 - core(), OWN - 1, two)


def residual_kernel(vec, own, previous, *rest):
    out, held, sems = rest[-3:]
    copies = []
    for j in range(4):
        held[j] = own[j] - previous[j]
        copies.append(pltpu.make_async_copy(held.at[j], out.at[0, vec, j], sems.at[j]))
        copies[-1].start()
    for copy in copies:
        copy.wait()


def shards(state, flow):
    rows, lanes = state.shape[-2:]
    slabs, segs = lax.axis_size("slab"), lax.axis_size("seg")
    near_pairs = [(i, i ^ 1) for i in range(slabs)]
    seg_pairs = [(i, (i + 1) % segs) for i in range(segs)]
    far_pairs = []
    for seg in range(segs):
        for slab in range(slabs):
            if slab in (0, slabs - 1):
                to = (seg ^ 2) * slabs + slab
            else:
                to = seg * slabs + (slab + 1 if slab % 2 else slab - 1)
            far_pairs.append((seg * slabs + slab, to))

    def far_swap(value):
        return lax.ppermute(value, ("seg", "slab"), far_pairs)

    def near_swap(value):
        return lax.ppermute(value, "slab", near_pairs)

    def planes(fields, count):
        return jax.ShapeDtypeStruct((fields, count, rows, lanes), F32)

    def scratch(fields, count):
        return pltpu.VMEM((fields, count, rows, lanes), F32)

    anywhere = pl.BlockSpec(memory_space=pl.ANY)
    vmem = pl.BlockSpec(memory_space=pltpu.VMEM)
    cost = pl.CostEstimate(flops=30_000_000, bytes_accessed=6_000_000, transcendentals=0)
    params = pltpu.CompilerParams(vmem_limit_bytes=16 * 1024 * 1024)

    def call(kernel, name, in_specs, out_shape, scratch_shapes, copies, **options):
        outs = out_shape if isinstance(out_shape, tuple) else (out_shape,)
        return pl.pallas_call(
            kernel,
            out_shape=out_shape,
            in_specs=in_specs,
            out_specs=options.pop("out_specs", (vmem,) * len(outs) if isinstance(out_shape, tuple) else vmem),
            scratch_shapes=scratch_shapes + [pltpu.SemaphoreType.DMA((copies,))],
            compiler_params=params,
            name=name,
            **options,
        )

    state_there = pltpu.with_memory_space_constraint(state, pltpu.HBM)
    flow_there = pltpu.with_memory_space_constraint(flow, pltpu.HBM)
    far_a, near = call(
        pack_kernel,
        "pack",
        [anywhere] * 2,
        (scratch(11, 1), scratch(11, HALO)),
        [scratch(4, 3), scratch(3, 3), scratch(COEFS, 1)],
        7,
    )(state_there, flow_there)
    far_a = far_swap(far_a)
    near = near_swap(near)

    coefs, own0, own1, *inner0 = call(
        inner_0_kernel,
        "inner_0",
        [anywhere] * 3,
        (planes(COEFS, COEF_PLANES), planes(4, OWN), planes(4, OWN), planes(4, OWN), planes(4, HALO), planes(4, HALO)),
        [scratch(4, WIDE), scratch(3, WIDE), scratch(4, WIDE)],
        6,
        cost_estimate=cost,
    )(state_there, flow_there, near)
    *inner1, far_b, near_mid = call(
        inner_1_kernel,
        "inner_1",
        [anywhere, anywhere, vmem, anywhere],
        (planes(4, OWN), planes(4, HALO), planes(4, HALO), planes(8, 1), planes(8, HALO)),
        [scratch(4, WIDE), scratch(4, WIDE)],
        3,
        cost_estimate=cost,
    )(own1, near, coefs, inner0[1])
    far_b = far_swap(far_b)
    near_mid = near_swap(near_mid)

    def first(vec, own, far_at, far_q, ready, *after):
        return call(
            functools.partial(first_kernel, far_at),
            f"first_{vec}",
            [anywhere, vmem] + [anywhere] * 7,
            (planes(4, OWN), planes(4, OWN), planes(8, 1)),
            [scratch(4, WIDE), scratch(4, WIDE), scratch(4, WIDE), scratch(4, 1), scratch(3, 1), scratch(3, 1)],
            7,
            cost_estimate=cost,
        )(own, coefs, far_a, far_q, *ready, *after)

    def second(vec, own, near_at, far_at, far_q, mid, part, far_mid, after):
        return call(
            functools.partial(second_kernel, near_at, far_at),
            f"second_{vec}",
            [anywhere, vmem] + [anywhere] * 4 + [vmem] + [anywhere] * 3,
            planes(4, OWN),
            [scratch(4, WIDE), scratch(4, WIDE), scratch(4, WIDE), scratch(4, 1), scratch(3, 1), scratch(3, 1)],
            8,
            cost_estimate=cost,
        )(own, coefs, near, far_a, far_q, mid, part, far_mid, near_mid, after)

    def residual(vec, own, previous, *buffer):
        return call(
            functools.partial(residual_kernel, vec),
            f"residual_{vec}",
            [vmem, vmem] + [anywhere] * vec,
            pltpu.HBM(state.shape, F32),
            [scratch(4, OWN)],
            4,
            out_specs=anywhere,
            input_output_aliases={2: 0} if vec else {},
        )(own, previous, *buffer)

    mid0, part0, far0 = first(0, own0, 3, far_a, inner0, inner1[1], inner1[1])
    far0 = far_swap(far0)
    mid1, part1, far1 = first(1, own1, 0, far_b, inner1, mid0, mid0)
    far1 = far_swap(far1)
    out0 = second(0, own0, 3, 3, far_a, mid0, part0, far0, mid1)
    prev0 = lax.ppermute(out0, "seg", seg_pairs)
    out1 = second(1, own1, 7, 0, far_b, mid1, part1, far1, out0)
    prev1 = lax.ppermute(out1, "seg", seg_pairs)
    advanced = jnp.stack([out0, out1])[None]
    return advanced, residual(1, own1, prev1, residual(0, own0, prev0))


def solution(mesh):
    return jax.shard_map(
        shards,
        mesh=mesh,
        in_specs=(P("seg", None, None, "slab", None, None), P("seg", None, "slab", None, None)),
        out_specs=(
            P("seg", None, None, "slab", None, None),
            P("seg", None, None, "slab", None, None),
        ),
        check_vma=False,
    )
```

time: 61.9 us -> 59.5 us (0.961)
  waiting for transfers between devices: 31.6 us -> 28.9 us
  Pallas kernels: 11.5 us -> 13.1 us
  other arithmetic: 2.26 us -> 1.08 us
    ppermute x4, waiting for transfers between devices: 17.4 us -> 11.3 us  [far_swap(): return lax.ppermute(value, ('seg', 'slab'), far_pairs)]
    ppermute x1, waiting for transfers between devices: 8.58 us -> 12.9 us  [shards(): prev0 = lax.ppermute(out0, 'seg', seg_pairs)]
    pallas_call x7 -> x9, Pallas kernels: 11.5 us -> 13.1 us  [the longest x2 3.95 us: second(): call(functools.partial(second_kernel, near_at, far_at), f'second_{vec}',...]
    broadcast_in_dim x1 -> x0, other arithmetic: 1.04 us -> none  [shards(): residual = jnp.stack([state[0, 0] - prev0, state[0, 1] - prev1])[None]]
    ppermute x1, waiting for transfers between devices: 5.62 us -> 4.7 us  [shards(): prev1 = lax.ppermute(out1, 'seg', seg_pairs)]
    ppermute x3 -> x2, starting transfers between devices: 2.01 us -> 1.5 us  [near_swap(): return lax.ppermute(value, 'slab', near_pairs)]
  transfers between devices with their start and end apart: 9 -> 8, of which waited for: 6 -> 6; matrix products, arithmetic and copies ran while one was open for 2% -> 2% of each run, Pallas kernels for 16% -> 18%
where the time goes in v1:
time: 59.5 us; the launch traced here: 59.3 us
  waiting for transfers between devices  28.9 us (49%)
  starting transfers between devices  15.5 us (26%)
  Pallas kernels  13.1 us (22%)
  other arithmetic  1.08 us (2%)
  between operations  0.7 us (1%)
    ppermute x4, starting transfers between devices, far_swap(): return lax.ppermute(value, ('seg', 'slab'), far_pairs)  13.3 us
    ppermute x1, waiting for transfers between devices, shards(): prev0 = lax.ppermute(out0, 'seg', seg_pairs)  12.9 us
    ppermute x4, waiting for transfers between devices, far_swap(): return lax.ppermute(value, ('seg', 'slab'), far_pairs)  11.3 us
    ppermute x1, waiting for transfers between devices, shards(): prev1 = lax.ppermute(out1, 'seg', seg_pairs)  4.7 us
    pallas_call x2, Pallas kernels, second(): call(functools.partial(second_kernel, near_at, far_at), f'second_{vec}',...  3.95 us
    pallas_call x1, Pallas kernels, shards(): call(inner_0_kernel, 'inner_0', [anywhere] * 3, (planes(COEFS, COEF_PLANE...  2.68 us
    pallas_call x2, Pallas kernels, first(): call(functools.partial(first_kernel, far_at), f'first_{vec}', [anywhere,...  2.2 us
    pallas_call x2, Pallas kernels, residual(): call(functools.partial(residual_kernel, vec), f'residual_{vec}', [vmem, v...  1.66 us
  transfers between devices with their start and end apart: 8, of which 6 were waited for; matrix products, arithmetic and copies ran while one was open for 2% of the time, Pallas kernels for 18%

profile of v1, /device:TPU:1, one launch (start us, length us, event | category | flops | bytes accessed | tf_op | source)
XLA Modules:
  0.0 59.3 jit_solution(16157643743999661975)
XLA Ops:
  0.6 1.4 %pack.1 = (f32[11,1,64,128]{3,2,1,0:T(8,128)S(1)}, f32[11,2,64,128]{3,2,1,0:T(8,128)S(1)}) custom-call(f32[1,2,4,4,64,128]{5,4,3,2,1,0:T(8,128)} %state.3, f32[1,3,4,64,128]{4,3,2,1,0:T(8,128)} %flow.3), custom_call_target="tpu_custom_call" | custom-call | tf_op jit(solution)/shard_map/pack/pallas_call | solution.py:400
  2.1 1.5 %collective-permute-start = (f32[11,2,64,128]{3,2,1,0:T(8,128)S(1)}, f32[11,2,64,128]{3,2,1,0:T(8,128)S(1)}, u32[]{:S(2)}, u32[]{:S(2)}) collective-permute-start(f32[11,2,64,128]{3,2,1,0:T(8,128)S(1)} %get-tuple-element.21), channel_id=1, source_target_pairs={{0,1},{1,0},{2,3},{3,2},{4,5},{5,4},{6,7},{7,6},{8,9},{9,8},{10,11... | collective-permute-start | bytes 2162696 | tf_op jit(solution)/shard_map/ppermute | solution.py:372
  3.6 3.0 %collective-permute-start.1 = (f32[11,1,64,128]{3,2,1,0:T(8,128)S(1)}, f32[11,1,64,128]{3,2,1,0:T(8,128)S(1)}, u32[]{:S(2)}, u32[]{:S(2)}) collective-permute-start(f32[11,1,64,128]{3,2,1,0:T(8,128)S(1)} %get-tuple-element.24), channel_id=1, source_target_pairs={{0,32},{1,2},{2,1},{3,4},{4,3},{5,6},{6,5},{7,8},{8,7},{9,10},{10,... | collective-permute-start | bytes 1081352 | tf_op jit(solution)/shard_map/ppermute | solution.py:369
  6.5 0.0 collective-permute-done.near
  6.6 2.7 %inner_0.1 = (f32[12,5,64,128]{3,2,1,0:T(8,128)S(1)}, f32[4,4,64,128]{3,2,1,0:T(8,128)S(1)}, f32[4,4,64,128]{3,2,1,0:T(8,128)S(1)}, f32[4,4,64,128]{3,2,1,0:T(8,...) custom-call(f32[1,2,4,4,64,128]{5,4,3,2,1,0:T(8,128)} %state.3, f32[1,3,4,64,128]{4,3,2,1,0:T(8,128)} %flow.3, ...), custom_call_target="tpu_custom_call" | custom-call | flops 30000000 | bytes 6000000 | tf_op jit(solution)/shard_map/inner_0/pallas_call | solution.py:411
  9.2 1.2 %inner_1.1 = (f32[4,4,64,128]{3,2,1,0:T(8,128)S(1)}, f32[4,2,64,128]{3,2,1,0:T(8,128)S(1)}, f32[4,2,64,128]{3,2,1,0:T(8,128)S(1)}, f32[8,1,64,128]{3,2,1,0:T(8,128)S(1)}, f32[8,2,64,128]{3,2,1,0:T(8,128)S(1)}) custom-call(f32[4,4,64,128]{3,2,1,0:T(8,128)S(1)} %get-tuple-element.28.own, f32[11,2,64,128]{3,2,1,0:T(8,128)S(1)} %collective-permute-done.near, ...), custom_call_target="tpu_custom_call" | custom-call | flops 30000000 | bytes 6000000 | tf_op jit(solution)/shard_map/inner_1/pallas_call | solution.py:420
  10.5 2.2 %collective-permute-start.4 = (f32[8,1,64,128]{3,2,1,0:T(8,128)S(1)}, f32[8,1,64,128]{3,2,1,0:T(8,128)S(1)}, u32[]{:S(2)}, u32[]{:S(2)}) collective-permute-start(f32[8,1,64,128]{3,2,1,0:T(8,128)S(1)} %get-tuple-element.34), channel_id=1, source_target_pairs={{0,32},{1,2},{2,1},{3,4},{4,3},{5,6},{6,5},{7,8},{8,7},{9,10},{10,... | collective-permute-start | bytes 786440 | tf_op jit(solution)/shard_map/ppermute | solution.py:369
  12.6 5.0 %collective-permute-done.1.far_a.far_q = f32[11,1,64,128]{3,2,1,0:T(8,128)S(1)} collective-permute-done((f32[11,1,64,128]{3,2,1,0:T(8,128)S(1)}, f32[11,1,64,128]{3,2,1,0:T(8,128)S(1)}, u32[]{:S(2)}, u32[]{:S(2)}) %collective-permute-start.1) | collective-permute-done | bytes 360480 | tf_op jit(solution)/shard_map/ppermute | solution.py:369
  17.6 1.1 %first_0.1 = (f32[4,4,64,128]{3,2,1,0:T(8,128)S(1)}, f32[4,4,64,128]{3,2,1,0:T(8,128)S(1)}, f32[8,1,64,128]{3,2,1,0:T(8,128)S(1)}) custom-call(f32[4,4,64,128]{3,2,1,0:T(8,128)S(1)} %get-tuple-element.22.own, f32[12,5,64,128]{3,2,1,0:T(8,128)S(1)} %get-tuple-element.23.coefs, f32[11,1,64,128]{3,2,1,0:T(8,128)S(1)} %collective-permute-done.1.far_a.far_q, ...), custom_call_target="tpu_custom_call" | custom-call | flops 30000000 | bytes 6000000 | tf_op jit(solution)/shard_map/first_0/pallas_call | solution.py:433
  18.7 4.1 %collective-permute-start.2 = (f32[8,1,64,128]{3,2,1,0:T(8,128)S(1)}, f32[8,1,64,128]{3,2,1,0:T(8,128)S(1)}, u32[]{:S(2)}, u32[]{:S(2)}) collective-permute-start(f32[8,1,64,128]{3,2,1,0:T(8,128)S(1)} %get-tuple-element.32), channel_id=1, source_target_pairs={{0,32},{1,2},{2,1},{3,4},{4,3},{5,6},{6,5},{7,8},{8,7},{9,10},{10,... | collective-permute-start | bytes 786440 | tf_op jit(solution)/shard_map/ppermute | solution.py:369
  22.8 0.4 collective-permute-done.4.far_q
  23.2 1.1 %first_1.1 = (f32[4,4,64,128]{3,2,1,0:T(8,128)S(1)}, f32[4,4,64,128]{3,2,1,0:T(8,128)S(1)}, f32[8,1,64,128]{3,2,1,0:T(8,128)S(1)}) custom-call(f32[4,4,64,128]{3,2,1,0:T(8,128)S(1)} %get-tuple-element.28.own, f32[12,5,64,128]{3,2,1,0:T(8,128)S(1)} %get-tuple-element.23.coefs, f32[11,1,64,128]{3,2,1,0:T(8,128)S(1)} %collective-permute-done.1.far_a.far_q, ...), custom_call_target="tpu_custom_call" | custom-call | flops 30000000 | bytes 6000000 | tf_op jit(solution)/shard_map/first_1/pallas_call | solution.py:433
  24.3 4.1 %collective-permute-start.5 = (f32[8,1,64,128]{3,2,1,0:T(8,128)S(1)}, f32[8,1,64,128]{3,2,1,0:T(8,128)S(1)}, u32[]{:S(2)}, u32[]{:S(2)}) collective-permute-start(f32[8,1,64,128]{3,2,1,0:T(8,128)S(1)} %get-tuple-element.39), channel_id=1, source_target_pairs={{0,32},{1,2},{2,1},{3,4},{4,3},{5,6},{6,5},{7,8},{8,7},{9,10},{10,... | collective-permute-start | bytes 786440 | tf_op jit(solution)/shard_map/ppermute | solution.py:369
  28.4 2.7 %collective-permute-done.2.far_mid = f32[8,1,64,128]{3,2,1,0:T(8,128)S(1)} collective-permute-done((f32[8,1,64,128]{3,2,1,0:T(8,128)S(1)}, f32[8,1,64,128]{3,2,1,0:T(8,128)S(1)}, u32[]{:S(2)}, u32[]{:S(2)}) %collective-permute-start.2) | collective-permute-done | bytes 262176 | tf_op jit(solution)/shard_map/ppermute | solution.py:369
  31.0 2.0 %second_0.1.after = f32[4,4,64,128]{3,2,1,0:T(8,128)S(1)} custom-call(f32[4,4,64,128]{3,2,1,0:T(8,128)S(1)} %get-tuple-element.22.own, f32[12,5,64,128]{3,2,1,0:T(8,128)S(1)} %get-tuple-element.23.coefs, f32[11,2,64,128]{3,2,1,0:T(8,128)S(1)} %collective-permute-done.near, f32[11,1,64,128]{3,2,1,0:T(8,128)S(1)} %collective-permute-done.1.far_a.far_q, ...), custom_call_target="tpu_custom_call" | custom-call | flops 30000000 | bytes 6000000 | tf_op jit(solution)/shard_map/second_0/pallas_call | solution.py:444
  33.0 0.3 collective-permute-start.7
  33.4 3.3 %collective-permute-done.5.far_mid = f32[8,1,64,128]{3,2,1,0:T(8,128)S(1)} collective-permute-done((f32[8,1,64,128]{3,2,1,0:T(8,128)S(1)}, f32[8,1,64,128]{3,2,1,0:T(8,128)S(1)}, u32[]{:S(2)}, u32[]{:S(2)}) %collective-permute-start.5) | collective-permute-done | bytes 262176 | tf_op jit(solution)/shard_map/ppermute | solution.py:369
  36.7 2.0 %second_1.1 = f32[4,4,64,128]{3,2,1,0:T(8,128)S(1)} custom-call(f32[4,4,64,128]{3,2,1,0:T(8,128)S(1)} %get-tuple-element.28.own, f32[12,5,64,128]{3,2,1,0:T(8,128)S(1)} %get-tuple-element.23.coefs, f32[11,2,64,128]{3,2,1,0:T(8,128)S(1)} %collective-permute-done.near, f32[11,1,64,128]{3,2,1,0:T(8,128)S(1)} %collective-permute-done.1.far_a.far_q, ...), custom_call_target="tpu_custom_call" | custom-call | flops 30000000 | bytes 6000000 | tf_op jit(solution)/shard_map/second_1/pallas_call | solution.py:444
  38.6 0.3 collective-permute-start.6
  39.0 1.1 %maximum_bitcast_fusion = f32[1,2,4,4,64,128]{5,4,3,2,1,0:T(8,128)} fusion(f32[1,4,4,64,128]{4,3,2,1,0:T(8,128)S(1)} %bitcast.5, f32[1,4,4,64,128]{4,3,2,1,0:T(8,128)S(1)} %bitcast.4), kind=kLoop, calls=%fused_computation | loop fusion | flops 262144 | bytes 2097152 | tf_op jit(solution)/shard_map/broadcast_in_dim | solution.py:474
  40.1 12.9 %collective-permute-done.7.previous = f32[4,4,64,128]{3,2,1,0:T(8,128)S(1)} collective-permute-done((f32[4,4,64,128]{3,2,1,0:T(8,128)S(1)}, f32[4,4,64,128]{3,2,1,0:T(8,128)S(1)}, u32[]{:S(2)}, u32[]{:S(2)}) %collective-permute-start.7) | collective-permute-done | bytes 524320 | tf_op jit(solution)/shard_map/ppermute | solution.py:471
  52.9 0.8 %residual_0.1.rest_0_ = f32[1,2,4,4,64,128]{5,4,3,2,1,0:T(8,128)} custom-call(f32[4,4,64,128]{3,2,1,0:T(8,128)S(1)} %get-tuple-element.22.own, f32[4,4,64,128]{3,2,1,0:T(8,128)S(1)} %collective-permute-done.7.previous), custom_call_target="tpu_custom_call" | custom-call | tf_op jit(solution)/shard_map/residual_0/pallas_call | solution.py:455
  53.8 4.7 %collective-permute-done.6.previous = f32[4,4,64,128]{3,2,1,0:T(8,128)S(1)} collective-permute-done((f32[4,4,64,128]{3,2,1,0:T(8,128)S(1)}, f32[4,4,64,128]{3,2,1,0:T(8,128)S(1)}, u32[]{:S(2)}, u32[]{:S(2)}) %collective-permute-start.6) | collective-permute-done | bytes 524320 | tf_op jit(solution)/shard_map/ppermute | solution.py:473
  58.5 0.8 %residual_1.1 = f32[1,2,4,4,64,128]{5,4,3,2,1,0:T(8,128)} custom-call(f32[4,4,64,128]{3,2,1,0:T(8,128)S(1)} %get-tuple-element.28.own, f32[4,4,64,128]{3,2,1,0:T(8,128)S(1)} %collective-permute-done.6.previous, f32[1,2,4,4,64,128]{5,4,3,2,1,0:T(8,128)} %residual_0.1.rest_0_), custom_call_target="tpu_custom_call", output_to_operand_aliasing={{}: (2, {})} | custom-call | tf_op jit(solution)/shard_map/residual_1/pallas_call | solution.py:455
  (2 shorter events, 0.0 us)
Async XLA Ops:
  2.1 4.5 %collective-permute-start = (f32[11,2,64,128]{3,2,1,0:T(8,128)S(1)}, f32[11,2,64,128]{3,2,1,0:T(8,128)S(1)}, u32[]{:S(2)}, u32[]{:S(2)}) collective-permute-start(f32[11,2,64,128]{3,2,1,0:T(8,128)S(1)} %get-tuple-element.21), channel_id=1, source_target_pairs={{0,1},{1,0},{2,3},{3,2},{4,5},{5,4},{6,7},{7,6},{8,9},{9,8},{10,11... | collective-permute-start | bytes 2162696 | tf_op jit(solution)/shard_map/ppermute | solution.py:372
  3.6 14.0 %collective-permute-start.1 = (f32[11,1,64,128]{3,2,1,0:T(8,128)S(1)}, f32[11,1,64,128]{3,2,1,0:T(8,128)S(1)}, u32[]{:S(2)}, u32[]{:S(2)}) collective-permute-start(f32[11,1,64,128]{3,2,1,0:T(8,128)S(1)} %get-tuple-element.24), channel_id=1, source_target_pairs={{0,32},{1,2},{2,1},{3,4},{4,3},{5,6},{6,5},{7,8},{8,7},{9,10},{10,... | collective-permute-start | bytes 1081352 | tf_op jit(solution)/shard_map/ppermute | solution.py:369
  10.5 12.7 %collective-permute-start.4 = (f32[8,1,64,128]{3,2,1,0:T(8,128)S(1)}, f32[8,1,64,128]{3,2,1,0:T(8,128)S(1)}, u32[]{:S(2)}, u32[]{:S(2)}) collective-permute-start(f32[8,1,64,128]{3,2,1,0:T(8,128)S(1)} %get-tuple-element.34), channel_id=1, source_target_pairs={{0,32},{1,2},{2,1},{3,4},{4,3},{5,6},{6,5},{7,8},{8,7},{9,10},{10,... | collective-permute-start | bytes 786440 | tf_op jit(solution)/shard_map/ppermute | solution.py:369
  12.6 18.4 %collective-permute-start.3 = (f32[8,2,64,128]{3,2,1,0:T(8,128)S(1)}, f32[8,2,64,128]{3,2,1,0:T(8,128)S(1)}, u32[]{:S(2)}, u32[]{:S(2)}) collective-permute-start(f32[8,2,64,128]{3,2,1,0:T(8,128)S(1)} %get-tuple-element.33), channel_id=1, source_target_pairs={{0,1},{1,0},{2,3},{3,2},{4,5},{5,4},{6,7},{7,6},{8,9},{9,8},{10,11... | collective-permute-start | bytes 1572872 | tf_op jit(solution)/shard_map/ppermute | solution.py:372
  18.7 12.3 %collective-permute-start.2 = (f32[8,1,64,128]{3,2,1,0:T(8,128)S(1)}, f32[8,1,64,128]{3,2,1,0:T(8,128)S(1)}, u32[]{:S(2)}, u32[]{:S(2)}) collective-permute-start(f32[8,1,64,128]{3,2,1,0:T(8,128)S(1)} %get-tuple-element.32), channel_id=1, source_target_pairs={{0,32},{1,2},{2,1},{3,4},{4,3},{5,6},{6,5},{7,8},{8,7},{9,10},{10,... | collective-permute-start | bytes 786440 | tf_op jit(solution)/shard_map/ppermute | solution.py:369
  24.3 12.3 %collective-permute-start.5 = (f32[8,1,64,128]{3,2,1,0:T(8,128)S(1)}, f32[8,1,64,128]{3,2,1,0:T(8,128)S(1)}, u32[]{:S(2)}, u32[]{:S(2)}) collective-permute-start(f32[8,1,64,128]{3,2,1,0:T(8,128)S(1)} %get-tuple-element.39), channel_id=1, source_target_pairs={{0,32},{1,2},{2,1},{3,4},{4,3},{5,6},{6,5},{7,8},{8,7},{9,10},{10,... | collective-permute-start | bytes 786440 | tf_op jit(solution)/shard_map/ppermute | solution.py:369
  33.0 19.9 %collective-permute-start.7 = (f32[4,4,64,128]{3,2,1,0:T(8,128)S(1)}, f32[4,4,64,128]{3,2,1,0:T(8,128)S(1)}, u32[]{:S(2)}, u32[]{:S(2)}) collective-permute-start(f32[4,4,64,128]{3,2,1,0:T(8,128)S(1)} %second_0.1.after), channel_id=1, source_target_pairs={{0,16},{16,32},{32,48},{48,64},{64,80},{80,96},{96,112},{112,0},{1... | collective-permute-start | bytes 1572872 | tf_op jit(solution)/shard_map/ppermute | solution.py:471
  38.6 19.8 %collective-permute-start.6 = (f32[4,4,64,128]{3,2,1,0:T(8,128)S(1)}, f32[4,4,64,128]{3,2,1,0:T(8,128)S(1)}, u32[]{:S(2)}, u32[]{:S(2)}) collective-permute-start(f32[4,4,64,128]{3,2,1,0:T(8,128)S(1)} %second_1.1), channel_id=1, source_target_pairs={{0,16},{16,32},{32,48},{48,64},{64,80},{80,96},{96,112},{112,0},{1... | collective-permute-start | bytes 1572872 | tf_op jit(solution)/shard_map/ppermute | solution.py:473

commit v2 on v1

--- a/solution.py
+++ b/solution.py
@@ -171,12 +171,10 @@
 
 
 def pack_kernel(state, flow, far_a, near, q, base, coefs, sems):
-    far, close, edge = core() * (OWN - HALO), (1 - core()) * (OWN - HALO), core() * (OWN - 1)
+    far, close = core() * (OWN - HALO), (1 - core()) * (OWN - HALO)
     pairs = [
         (flow.at[0, :, pl.ds(far, HALO)], base.at[:, pl.ds(1 - core(), HALO)]),
         (state.at[0, 0, :, pl.ds(far, HALO)], q.at[:, pl.ds(1 - core(), HALO)]),
-        (flow.at[0, :, pl.ds(edge, 1)], far_a.at[0:3]),
-        (state.at[0, 0, :, pl.ds(edge, 1)], far_a.at[3:7]),
         (flow.at[0, :, pl.ds(close, HALO)], near.at[0:3]),
         (state.at[0, 0, :, pl.ds(close, HALO)], near.at[3:7]),
         (state.at[0, 1, :, pl.ds(close, HALO)], near.at[7:11]),
@@ -188,7 +186,9 @@
     rows = q.shape[2]
     for row in range(0, rows, TILE):
         tile_coefs(base, 1, coefs, 0, row, rows)
+    far_a[0:3] = base[:, 1:2]
     copies[1].wait()
+    far_a[3:7] = q[:, 1:2]
     partial_rates(q, coefs, 1, 0, far_a, 7)
     for copy in copies[2:]:
         copy.wait()
@@ -340,6 +340,11 @@
     over_rates(fourth, coefs, 3 - core(), OWN - 1, two)
 
 
+def hold_kernel(value, after, out, sems):
+    del after
+    run_copies([(value, out)], sems)
+
+
 def residual_kernel(vec, own, previous, *rest):
     out, held, sems = rest[-3:]
     copies = []
@@ -403,10 +408,10 @@
         [anywhere] * 2,
         (scratch(11, 1), scratch(11, HALO)),
         [scratch(4, 3), scratch(3, 3), scratch(COEFS, 1)],
-        7,
+        5,
     )(state_there, flow_there)
+    near = near_swap(near)
     far_a = far_swap(far_a)
-    near = near_swap(near)
 
     coefs, own0, own1, *inner0 = call(
         inner_0_kernel,
@@ -468,7 +473,8 @@
     mid1, part1, far1 = first(1, own1, 0, far_b, inner1, mid0, mid0)
     far1 = far_swap(far1)
     out0 = second(0, own0, 3, 3, far_a, mid0, part0, far0, mid1)
-    prev0 = lax.ppermute(out0, "seg", seg_pairs)
+    held0 = call(hold_kernel, "hold", [anywhere] * 2, scratch(4, OWN), [], 1)(out0, far1)
+    prev0 = lax.ppermute(held0, "seg", seg_pairs)
     out1 = second(1, own1, 7, 0, far_b, mid1, part1, far1, out0)
     prev1 = lax.ppermute(out1, "seg", seg_pairs)
     advanced = jnp.stack([out0, out1])[None]

time: 59.5 us -> 59.4 us (level)
  waiting for transfers between devices: 28.9 us -> 26.6 us
  starting transfers between devices: 15.5 us -> 17.7 us
    ppermute x1, starting transfers between devices: 0.34 us -> 2.86 us  [shards(): prev1 = lax.ppermute(out1, 'seg', seg_pairs)]
    ppermute x1, waiting for transfers between devices: 12.9 us -> 10.4 us  [shards(): prev0 = lax.ppermute(held0, 'seg', seg_pairs)]
where the time goes in v2:
time: 59.4 us; the launch traced here: 59.2 us
  waiting for transfers between devices  26.6 us (45%)
  starting transfers between devices  17.7 us (30%)
  Pallas kernels  13.1 us (22%)
  other arithmetic  1.08 us (2%)
  between operations  0.72 us (1%)
    ppermute x4, starting transfers between devices, far_swap(): return lax.ppermute(value, ('seg', 'slab'), far_pairs)  13.3 us
    ppermute x4, waiting for transfers between devices, far_swap(): return lax.ppermute(value, ('seg', 'slab'), far_pairs)  11.6 us
    ppermute x1, waiting for transfers between devices, shards(): prev0 = lax.ppermute(held0, 'seg', seg_pairs)  10.4 us
    ppermute x1, waiting for transfers between devices, shards(): prev1 = lax.ppermute(out1, 'seg', seg_pairs)  4.57 us
    pallas_call x2, Pallas kernels, second(): call(functools.partial(second_kernel, near_at, far_at), f'second_{vec}',...  3.97 us
    ppermute x1, starting transfers between devices, shards(): prev1 = lax.ppermute(out1, 'seg', seg_pairs)  2.86 us
    pallas_call x1, Pallas kernels, shards(): call(inner_0_kernel, 'inner_0', [anywhere] * 3, (planes(COEFS, COEF_PLANE...  2.68 us
    pallas_call x2, Pallas kernels, first(): call(functools.partial(first_kernel, far_at), f'first_{vec}', [anywhere,...  2.2 us
  transfers between devices with their start and end apart: 8, of which 6 were waited for; matrix products, arithmetic and copies ran while one was open for 2% of the time, Pallas kernels for 18%

profile of v2, /device:TPU:1, one launch (start us, length us, event | category | flops | bytes accessed | tf_op | source)
XLA Modules:
  0.0 59.2 jit_solution(7191465509633868663)
XLA Ops:
  0.6 1.4 %pack.1 = (f32[11,1,64,128]{3,2,1,0:T(8,128)S(1)}, f32[11,2,64,128]{3,2,1,0:T(8,128)S(1)}) custom-call(f32[1,2,4,4,64,128]{5,4,3,2,1,0:T(8,128)} %state.3, f32[1,3,4,64,128]{4,3,2,1,0:T(8,128)} %flow.3), custom_call_target="tpu_custom_call" | custom-call | tf_op jit(solution)/shard_map/pack/pallas_call | solution.py:405
  2.0 1.5 %collective-permute-start = (f32[11,2,64,128]{3,2,1,0:T(8,128)S(1)}, f32[11,2,64,128]{3,2,1,0:T(8,128)S(1)}, u32[]{:S(2)}, u32[]{:S(2)}) collective-permute-start(f32[11,2,64,128]{3,2,1,0:T(8,128)S(1)} %get-tuple-element.21), channel_id=1, source_target_pairs={{0,1},{1,0},{2,3},{3,2},{4,5},{5,4},{6,7},{7,6},{8,9},{9,8},{10,11... | collective-permute-start | bytes 2162696 | tf_op jit(solution)/shard_map/ppermute | solution.py:377
  3.5 3.0 %collective-permute-start.1 = (f32[11,1,64,128]{3,2,1,0:T(8,128)S(1)}, f32[11,1,64,128]{3,2,1,0:T(8,128)S(1)}, u32[]{:S(2)}, u32[]{:S(2)}) collective-permute-start(f32[11,1,64,128]{3,2,1,0:T(8,128)S(1)} %get-tuple-element.24), channel_id=1, source_target_pairs={{0,32},{1,2},{2,1},{3,4},{4,3},{5,6},{6,5},{7,8},{8,7},{9,10},{10,... | collective-permute-start | bytes 1081352 | tf_op jit(solution)/shard_map/ppermute | solution.py:374
  6.5 0.0 collective-permute-done.near
  6.5 2.7 %inner_0.1 = (f32[12,5,64,128]{3,2,1,0:T(8,128)S(1)}, f32[4,4,64,128]{3,2,1,0:T(8,128)S(1)}, f32[4,4,64,128]{3,2,1,0:T(8,128)S(1)}, f32[4,4,64,128]{3,2,1,0:T(8,...) custom-call(f32[1,2,4,4,64,128]{5,4,3,2,1,0:T(8,128)} %state.3, f32[1,3,4,64,128]{4,3,2,1,0:T(8,128)} %flow.3, ...), custom_call_target="tpu_custom_call" | custom-call | flops 30000000 | bytes 6000000 | tf_op jit(solution)/shard_map/inner_0/pallas_call | solution.py:416
  9.2 1.2 %inner_1.1 = (f32[4,4,64,128]{3,2,1,0:T(8,128)S(1)}, f32[4,2,64,128]{3,2,1,0:T(8,128)S(1)}, f32[4,2,64,128]{3,2,1,0:T(8,128)S(1)}, f32[8,1,64,128]{3,2,1,0:T(8,128)S(1)}, f32[8,2,64,128]{3,2,1,0:T(8,128)S(1)}) custom-call(f32[4,4,64,128]{3,2,1,0:T(8,128)S(1)} %get-tuple-element.28.own, f32[11,2,64,128]{3,2,1,0:T(8,128)S(1)} %collective-permute-done.near, ...), custom_call_target="tpu_custom_call" | custom-call | flops 30000000 | bytes 6000000 | tf_op jit(solution)/shard_map/inner_1/pallas_call | solution.py:425
  10.4 2.2 %collective-permute-start.4 = (f32[8,1,64,128]{3,2,1,0:T(8,128)S(1)}, f32[8,1,64,128]{3,2,1,0:T(8,128)S(1)}, u32[]{:S(2)}, u32[]{:S(2)}) collective-permute-start(f32[8,1,64,128]{3,2,1,0:T(8,128)S(1)} %get-tuple-element.34), channel_id=1, source_target_pairs={{0,32},{1,2},{2,1},{3,4},{4,3},{5,6},{6,5},{7,8},{8,7},{9,10},{10,... | collective-permute-start | bytes 786440 | tf_op jit(solution)/shard_map/ppermute | solution.py:374
  12.6 5.0 %collective-permute-done.1.far_a.far_q = f32[11,1,64,128]{3,2,1,0:T(8,128)S(1)} collective-permute-done((f32[11,1,64,128]{3,2,1,0:T(8,128)S(1)}, f32[11,1,64,128]{3,2,1,0:T(8,128)S(1)}, u32[]{:S(2)}, u32[]{:S(2)}) %collective-permute-start.1) | collective-permute-done | bytes 360480 | tf_op jit(solution)/shard_map/ppermute | solution.py:374
  17.5 1.1 %first_0.1 = (f32[4,4,64,128]{3,2,1,0:T(8,128)S(1)}, f32[4,4,64,128]{3,2,1,0:T(8,128)S(1)}, f32[8,1,64,128]{3,2,1,0:T(8,128)S(1)}) custom-call(f32[4,4,64,128]{3,2,1,0:T(8,128)S(1)} %get-tuple-element.22.own, f32[12,5,64,128]{3,2,1,0:T(8,128)S(1)} %get-tuple-element.23.coefs, f32[11,1,64,128]{3,2,1,0:T(8,128)S(1)} %collective-permute-done.1.far_a.far_q, ...), custom_call_target="tpu_custom_call" | custom-call | flops 30000000 | bytes 6000000 | tf_op jit(solution)/shard_map/first_0/pallas_call | solution.py:438
  18.6 4.1 %collective-permute-start.2 = (f32[8,1,64,128]{3,2,1,0:T(8,128)S(1)}, f32[8,1,64,128]{3,2,1,0:T(8,128)S(1)}, u32[]{:S(2)}, u32[]{:S(2)}) collective-permute-start(f32[8,1,64,128]{3,2,1,0:T(8,128)S(1)} %get-tuple-element.32), channel_id=1, source_target_pairs={{0,32},{1,2},{2,1},{3,4},{4,3},{5,6},{6,5},{7,8},{8,7},{9,10},{10,... | collective-permute-start | bytes 786440 | tf_op jit(solution)/shard_map/ppermute | solution.py:374
  22.7 0.4 collective-permute-done.4.far_q
  23.1 1.1 %first_1.1 = (f32[4,4,64,128]{3,2,1,0:T(8,128)S(1)}, f32[4,4,64,128]{3,2,1,0:T(8,128)S(1)}, f32[8,1,64,128]{3,2,1,0:T(8,128)S(1)}) custom-call(f32[4,4,64,128]{3,2,1,0:T(8,128)S(1)} %get-tuple-element.28.own, f32[12,5,64,128]{3,2,1,0:T(8,128)S(1)} %get-tuple-element.23.coefs, f32[11,1,64,128]{3,2,1,0:T(8,128)S(1)} %collective-permute-done.1.far_a.far_q, ...), custom_call_target="tpu_custom_call" | custom-call | flops 30000000 | bytes 6000000 | tf_op jit(solution)/shard_map/first_1/pallas_call | solution.py:438
  24.2 4.1 %collective-permute-start.5 = (f32[8,1,64,128]{3,2,1,0:T(8,128)S(1)}, f32[8,1,64,128]{3,2,1,0:T(8,128)S(1)}, u32[]{:S(2)}, u32[]{:S(2)}) collective-permute-start(f32[8,1,64,128]{3,2,1,0:T(8,128)S(1)} %get-tuple-element.39), channel_id=1, source_target_pairs={{0,32},{1,2},{2,1},{3,4},{4,3},{5,6},{6,5},{7,8},{8,7},{9,10},{10,... | collective-permute-start | bytes 786440 | tf_op jit(solution)/shard_map/ppermute | solution.py:374
  28.3 2.6 %collective-permute-done.2.far_mid = f32[8,1,64,128]{3,2,1,0:T(8,128)S(1)} collective-permute-done((f32[8,1,64,128]{3,2,1,0:T(8,128)S(1)}, f32[8,1,64,128]{3,2,1,0:T(8,128)S(1)}, u32[]{:S(2)}, u32[]{:S(2)}) %collective-permute-start.2) | collective-permute-done | bytes 262176 | tf_op jit(solution)/shard_map/ppermute | solution.py:374
  30.9 2.0 %second_0.1.after.value = f32[4,4,64,128]{3,2,1,0:T(8,128)S(1)} custom-call(f32[4,4,64,128]{3,2,1,0:T(8,128)S(1)} %get-tuple-element.22.own, f32[12,5,64,128]{3,2,1,0:T(8,128)S(1)} %get-tuple-element.23.coefs, f32[11,2,64,128]{3,2,1,0:T(8,128)S(1)} %collective-permute-done.near, f32[11,1,64,128]{3,2,1,0:T(8,128)S(1)} %collective-permute-done.1.far_a.far_q, ...), custom_call_target="tpu_custom_call" | custom-call | flops 30000000 | bytes 6000000 | tf_op jit(solution)/shard_map/second_0/pallas_call | solution.py:449
  32.9 3.6 %collective-permute-done.5.far_mid.after = f32[8,1,64,128]{3,2,1,0:T(8,128)S(1)} collective-permute-done((f32[8,1,64,128]{3,2,1,0:T(8,128)S(1)}, f32[8,1,64,128]{3,2,1,0:T(8,128)S(1)}, u32[]{:S(2)}, u32[]{:S(2)}) %collective-permute-start.5) | collective-permute-done | bytes 262176 | tf_op jit(solution)/shard_map/ppermute | solution.py:374
  36.6 0.1 collective-permute-start.7
  36.6 2.0 %second_1.1 = f32[4,4,64,128]{3,2,1,0:T(8,128)S(1)} custom-call(f32[4,4,64,128]{3,2,1,0:T(8,128)S(1)} %get-tuple-element.28.own, f32[12,5,64,128]{3,2,1,0:T(8,128)S(1)} %get-tuple-element.23.coefs, f32[11,2,64,128]{3,2,1,0:T(8,128)S(1)} %collective-permute-done.near, f32[11,1,64,128]{3,2,1,0:T(8,128)S(1)} %collective-permute-done.1.far_a.far_q, ...), custom_call_target="tpu_custom_call" | custom-call | flops 30000000 | bytes 6000000 | tf_op jit(solution)/shard_map/second_1/pallas_call | solution.py:449
  38.6 2.9 %collective-permute-start.6 = (f32[4,4,64,128]{3,2,1,0:T(8,128)S(1)}, f32[4,4,64,128]{3,2,1,0:T(8,128)S(1)}, u32[]{:S(2)}, u32[]{:S(2)}) collective-permute-start(f32[4,4,64,128]{3,2,1,0:T(8,128)S(1)} %second_1.1), channel_id=1, source_target_pairs={{0,16},{16,32},{32,48},{48,64},{64,80},{80,96},{96,112},{112,0},{1... | collective-permute-start | bytes 1572872 | tf_op jit(solution)/shard_map/ppermute | solution.py:479
  41.5 1.1 %maximum_bitcast_fusion = f32[1,2,4,4,64,128]{5,4,3,2,1,0:T(8,128)} fusion(f32[1,4,4,64,128]{4,3,2,1,0:T(8,128)S(1)} %bitcast.5, f32[1,4,4,64,128]{4,3,2,1,0:T(8,128)S(1)} %bitcast.4), kind=kLoop, calls=%fused_computation | loop fusion | flops 262144 | bytes 2097152 | tf_op jit(solution)/shard_map/broadcast_in_dim | solution.py:480
  42.6 10.4 %collective-permute-done.7.previous = f32[4,4,64,128]{3,2,1,0:T(8,128)S(1)} collective-permute-done((f32[4,4,64,128]{3,2,1,0:T(8,128)S(1)}, f32[4,4,64,128]{3,2,1,0:T(8,128)S(1)}, u32[]{:S(2)}, u32[]{:S(2)}) %collective-permute-start.7) | collective-permute-done | bytes 524320 | tf_op jit(solution)/shard_map/ppermute | solution.py:477
  53.0 0.8 %residual_0.1.rest_0_ = f32[1,2,4,4,64,128]{5,4,3,2,1,0:T(8,128)} custom-call(f32[4,4,64,128]{3,2,1,0:T(8,128)S(1)} %get-tuple-element.22.own, f32[4,4,64,128]{3,2,1,0:T(8,128)S(1)} %collective-permute-done.7.previous), custom_call_target="tpu_custom_call" | custom-call | tf_op jit(solution)/shard_map/residual_0/pallas_call | solution.py:460
  53.8 4.6 %collective-permute-done.6.previous = f32[4,4,64,128]{3,2,1,0:T(8,128)S(1)} collective-permute-done((f32[4,4,64,128]{3,2,1,0:T(8,128)S(1)}, f32[4,4,64,128]{3,2,1,0:T(8,128)S(1)}, u32[]{:S(2)}, u32[]{:S(2)}) %collective-permute-start.6) | collective-permute-done | bytes 524320 | tf_op jit(solution)/shard_map/ppermute | solution.py:479
  58.4 0.8 %residual_1.1 = f32[1,2,4,4,64,128]{5,4,3,2,1,0:T(8,128)} custom-call(f32[4,4,64,128]{3,2,1,0:T(8,128)S(1)} %get-tuple-element.28.own, f32[4,4,64,128]{3,2,1,0:T(8,128)S(1)} %collective-permute-done.6.previous, f32[1,2,4,4,64,128]{5,4,3,2,1,0:T(8,128)} %residual_0.1.rest_0_), custom_call_target="tpu_custom_call", output_to_operand_aliasing={{}: (2, {})} | custom-call | tf_op jit(solution)/shard_map/residual_1/pallas_call | solution.py:460
  (3 shorter events, 0.1 us)
Async XLA Ops:
  2.0 4.5 %collective-permute-start = (f32[11,2,64,128]{3,2,1,0:T(8,128)S(1)}, f32[11,2,64,128]{3,2,1,0:T(8,128)S(1)}, u32[]{:S(2)}, u32[]{:S(2)}) collective-permute-start(f32[11,2,64,128]{3,2,1,0:T(8,128)S(1)} %get-tuple-element.21), channel_id=1, source_target_pairs={{0,1},{1,0},{2,3},{3,2},{4,5},{5,4},{6,7},{7,6},{8,9},{9,8},{10,11... | collective-permute-start | bytes 2162696 | tf_op jit(solution)/shard_map/ppermute | solution.py:377
  3.5 14.0 %collective-permute-start.1 = (f32[11,1,64,128]{3,2,1,0:T(8,128)S(1)}, f32[11,1,64,128]{3,2,1,0:T(8,128)S(1)}, u32[]{:S(2)}, u32[]{:S(2)}) collective-permute-start(f32[11,1,64,128]{3,2,1,0:T(8,128)S(1)} %get-tuple-element.24), channel_id=1, source_target_pairs={{0,32},{1,2},{2,1},{3,4},{4,3},{5,6},{6,5},{7,8},{8,7},{9,10},{10,... | collective-permute-start | bytes 1081352 | tf_op jit(solution)/shard_map/ppermute | solution.py:374
  10.4 12.7 %collective-permute-start.4 = (f32[8,1,64,128]{3,2,1,0:T(8,128)S(1)}, f32[8,1,64,128]{3,2,1,0:T(8,128)S(1)}, u32[]{:S(2)}, u32[]{:S(2)}) collective-permute-start(f32[8,1,64,128]{3,2,1,0:T(8,128)S(1)} %get-tuple-element.34), channel_id=1, source_target_pairs={{0,32},{1,2},{2,1},{3,4},{4,3},{5,6},{6,5},{7,8},{8,7},{9,10},{10,... | collective-permute-start | bytes 786440 | tf_op jit(solution)/shard_map/ppermute | solution.py:374
  12.6 18.3 %collective-permute-start.3 = (f32[8,2,64,128]{3,2,1,0:T(8,128)S(1)}, f32[8,2,64,128]{3,2,1,0:T(8,128)S(1)}, u32[]{:S(2)}, u32[]{:S(2)}) collective-permute-start(f32[8,2,64,128]{3,2,1,0:T(8,128)S(1)} %get-tuple-element.33), channel_id=1, source_target_pairs={{0,1},{1,0},{2,3},{3,2},{4,5},{5,4},{6,7},{7,6},{8,9},{9,8},{10,11... | collective-permute-start | bytes 1572872 | tf_op jit(solution)/shard_map/ppermute | solution.py:377
  18.6 12.3 %collective-permute-start.2 = (f32[8,1,64,128]{3,2,1,0:T(8,128)S(1)}, f32[8,1,64,128]{3,2,1,0:T(8,128)S(1)}, u32[]{:S(2)}, u32[]{:S(2)}) collective-permute-start(f32[8,1,64,128]{3,2,1,0:T(8,128)S(1)} %get-tuple-element.32), channel_id=1, source_target_pairs={{0,32},{1,2},{2,1},{3,4},{4,3},{5,6},{6,5},{7,8},{8,7},{9,10},{10,... | collective-permute-start | bytes 786440 | tf_op jit(solution)/shard_map/ppermute | solution.py:374
  24.2 12.3 %collective-permute-start.5 = (f32[8,1,64,128]{3,2,1,0:T(8,128)S(1)}, f32[8,1,64,128]{3,2,1,0:T(8,128)S(1)}, u32[]{:S(2)}, u32[]{:S(2)}) collective-permute-start(f32[8,1,64,128]{3,2,1,0:T(8,128)S(1)} %get-tuple-element.39), channel_id=1, source_target_pairs={{0,32},{1,2},{2,1},{3,4},{4,3},{5,6},{6,5},{7,8},{8,7},{9,10},{10,... | collective-permute-start | bytes 786440 | tf_op jit(solution)/shard_map/ppermute | solution.py:374
  36.6 16.4 %collective-permute-start.7 = (f32[4,4,64,128]{3,2,1,0:T(8,128)S(1)}, f32[4,4,64,128]{3,2,1,0:T(8,128)S(1)}, u32[]{:S(2)}, u32[]{:S(2)}) collective-permute-start(f32[4,4,64,128]{3,2,1,0:T(8,128)S(1)} %hold.1), channel_id=1, source_target_pairs={{0,16},{16,32},{32,48},{48,64},{64,80},{80,96},{96,112},{112,0},{1... | collective-permute-start | bytes 1572872 | tf_op jit(solution)/shard_map/ppermute | solution.py:477
  38.6 19.8 %collective-permute-start.6 = (f32[4,4,64,128]{3,2,1,0:T(8,128)S(1)}, f32[4,4,64,128]{3,2,1,0:T(8,128)S(1)}, u32[]{:S(2)}, u32[]{:S(2)}) collective-permute-start(f32[4,4,64,128]{3,2,1,0:T(8,128)S(1)} %second_1.1), channel_id=1, source_target_pairs={{0,16},{16,32},{32,48},{48,64},{64,80},{80,96},{96,112},{112,0},{1... | collective-permute-start | bytes 1572872 | tf_op jit(solution)/shard_map/ppermute | solution.py:479

commit v3 on v2

--- a/solution.py
+++ b/solution.py
@@ -171,27 +171,26 @@
 
 
 def pack_kernel(state, flow, far_a, near, q, base, coefs, sems):
-    far, close = core() * (OWN - HALO), (1 - core()) * (OWN - HALO)
+    close, edge = (1 - core()) * (OWN - HALO), 1 + core() * (OWN - 1)
     pairs = [
-        (flow.at[0, :, pl.ds(far, HALO)], base.at[:, pl.ds(1 - core(), HALO)]),
-        (state.at[0, 0, :, pl.ds(far, HALO)], q.at[:, pl.ds(1 - core(), HALO)]),
-        (flow.at[0, :, pl.ds(close, HALO)], near.at[0:3]),
-        (state.at[0, 0, :, pl.ds(close, HALO)], near.at[3:7]),
+        (flow.at[0], base.at[:, 1 : 1 + OWN]),
+        (state.at[0, 0], q.at[:, 1 : 1 + OWN]),
         (state.at[0, 1, :, pl.ds(close, HALO)], near.at[7:11]),
     ]
     copies = start_copies(pairs, sems)
-    zero_planes(q, 2 * core(), 1)
-    zero_planes(base, 2 * core(), 1)
+    zero_planes(q, core() * (OWN + 1), 1)
+    zero_planes(base, core() * (OWN + 1), 1)
     copies[0].wait()
     rows = q.shape[2]
     for row in range(0, rows, TILE):
-        tile_coefs(base, 1, coefs, 0, row, rows)
-    far_a[0:3] = base[:, 1:2]
+        tile_coefs(base, edge, coefs, 0, row, rows)
+    far_a[0:3] = base[:, pl.ds(edge, 1)]
+    near[0:3] = base[:, pl.ds(1 + close, HALO)]
     copies[1].wait()
-    far_a[3:7] = q[:, 1:2]
-    partial_rates(q, coefs, 1, 0, far_a, 7)
-    for copy in copies[2:]:
-        copy.wait()
+    far_a[3:7] = q[:, pl.ds(edge, 1)]
+    near[3:7] = q[:, pl.ds(1 + close, HALO)]
+    partial_rates(q, coefs, edge, 0, far_a, 7)
+    copies[2].wait()
 
 
 def inner_stages(q, coefs, second, second_out, mid, part):
@@ -407,8 +406,8 @@
         "pack",
         [anywhere] * 2,
         (scratch(11, 1), scratch(11, HALO)),
-        [scratch(4, 3), scratch(3, 3), scratch(COEFS, 1)],
-        5,
+        [scratch(4, OWN + 2), scratch(3, OWN + 2), scratch(COEFS, 1)],
+        3,
     )(state_there, flow_there)
     near = near_swap(near)
     far_a = far_swap(far_a)

time: 59.4 us -> 59.4 us (level)
  no operation moved by 1% of the time
where the time goes in v3:
time: 59.4 us; the launch traced here: 59.2 us
  waiting for transfers between devices  26.6 us (45%)
  starting transfers between devices  17.7 us (30%)
  Pallas kernels  13.1 us (22%)
  other arithmetic  1.08 us (2%)
  between operations  0.72 us (1%)
    ppermute x4, starting transfers between devices, far_swap(): return lax.ppermute(value, ('seg', 'slab'), far_pairs)  13.3 us
    ppermute x4, waiting for transfers between devices, far_swap(): return lax.ppermute(value, ('seg', 'slab'), far_pairs)  11.6 us
    ppermute x1, waiting for transfers between devices, shards(): prev0 = lax.ppermute(held0, 'seg', seg_pairs)  10.4 us
    ppermute x1, waiting for transfers between devices, shards(): prev1 = lax.ppermute(out1, 'seg', seg_pairs)  4.57 us
    pallas_call x2, Pallas kernels, second(): call(functools.partial(second_kernel, near_at, far_at), f'second_{vec}',...  3.97 us
    ppermute x1, starting transfers between devices, shards(): prev1 = lax.ppermute(out1, 'seg', seg_pairs)  2.86 us
    pallas_call x1, Pallas kernels, shards(): call(inner_0_kernel, 'inner_0', [anywhere] * 3, (planes(COEFS, COEF_PLANE...  2.68 us
    pallas_call x2, Pallas kernels, first(): call(functools.partial(first_kernel, far_at), f'first_{vec}', [anywhere,...  2.2 us
  transfers between devices with their start and end apart: 8, of which 6 were waited for; matrix products, arithmetic and copies ran while one was open for 2% of the time, Pallas kernels for 18%

profile of v3, /device:TPU:1, one launch (start us, length us, event | category | flops | bytes accessed | tf_op | source)
XLA Modules:
  0.0 59.2 jit_solution(13270715988168453998)
XLA Ops:
  0.6 1.4 %pack.1 = (f32[11,1,64,128]{3,2,1,0:T(8,128)S(1)}, f32[11,2,64,128]{3,2,1,0:T(8,128)S(1)}) custom-call(f32[1,2,4,4,64,128]{5,4,3,2,1,0:T(8,128)} %state.3, f32[1,3,4,64,128]{4,3,2,1,0:T(8,128)} %flow.3), custom_call_target="tpu_custom_call" | custom-call | tf_op jit(solution)/shard_map/pack/pallas_call | solution.py:404
  2.0 1.5 %collective-permute-start = (f32[11,2,64,128]{3,2,1,0:T(8,128)S(1)}, f32[11,2,64,128]{3,2,1,0:T(8,128)S(1)}, u32[]{:S(2)}, u32[]{:S(2)}) collective-permute-start(f32[11,2,64,128]{3,2,1,0:T(8,128)S(1)} %get-tuple-element.21), channel_id=1, source_target_pairs={{0,1},{1,0},{2,3},{3,2},{4,5},{5,4},{6,7},{7,6},{8,9},{9,8},{10,11... | collective-permute-start | bytes 2162696 | tf_op jit(solution)/shard_map/ppermute | solution.py:376
  3.5 3.0 %collective-permute-start.1 = (f32[11,1,64,128]{3,2,1,0:T(8,128)S(1)}, f32[11,1,64,128]{3,2,1,0:T(8,128)S(1)}, u32[]{:S(2)}, u32[]{:S(2)}) collective-permute-start(f32[11,1,64,128]{3,2,1,0:T(8,128)S(1)} %get-tuple-element.24), channel_id=1, source_target_pairs={{0,32},{1,2},{2,1},{3,4},{4,3},{5,6},{6,5},{7,8},{8,7},{9,10},{10,... | collective-permute-start | bytes 1081352 | tf_op jit(solution)/shard_map/ppermute | solution.py:373
  6.5 0.0 collective-permute-done.near
  6.5 2.7 %inner_0.1 = (f32[12,5,64,128]{3,2,1,0:T(8,128)S(1)}, f32[4,4,64,128]{3,2,1,0:T(8,128)S(1)}, f32[4,4,64,128]{3,2,1,0:T(8,128)S(1)}, f32[4,4,64,128]{3,2,1,0:T(8,...) custom-call(f32[1,2,4,4,64,128]{5,4,3,2,1,0:T(8,128)} %state.3, f32[1,3,4,64,128]{4,3,2,1,0:T(8,128)} %flow.3, ...), custom_call_target="tpu_custom_call" | custom-call | flops 30000000 | bytes 6000000 | tf_op jit(solution)/shard_map/inner_0/pallas_call | solution.py:415
  9.2 1.2 %inner_1.1 = (f32[4,4,64,128]{3,2,1,0:T(8,128)S(1)}, f32[4,2,64,128]{3,2,1,0:T(8,128)S(1)}, f32[4,2,64,128]{3,2,1,0:T(8,128)S(1)}, f32[8,1,64,128]{3,2,1,0:T(8,128)S(1)}, f32[8,2,64,128]{3,2,1,0:T(8,128)S(1)}) custom-call(f32[4,4,64,128]{3,2,1,0:T(8,128)S(1)} %get-tuple-element.28.own, f32[11,2,64,128]{3,2,1,0:T(8,128)S(1)} %collective-permute-done.near, ...), custom_call_target="tpu_custom_call" | custom-call | flops 30000000 | bytes 6000000 | tf_op jit(solution)/shard_map/inner_1/pallas_call | solution.py:424
  10.4 2.2 %collective-permute-start.4 = (f32[8,1,64,128]{3,2,1,0:T(8,128)S(1)}, f32[8,1,64,128]{3,2,1,0:T(8,128)S(1)}, u32[]{:S(2)}, u32[]{:S(2)}) collective-permute-start(f32[8,1,64,128]{3,2,1,0:T(8,128)S(1)} %get-tuple-element.34), channel_id=1, source_target_pairs={{0,32},{1,2},{2,1},{3,4},{4,3},{5,6},{6,5},{7,8},{8,7},{9,10},{10,... | collective-permute-start | bytes 786440 | tf_op jit(solution)/shard_map/ppermute | solution.py:373
  12.6 5.0 %collective-permute-done.1.far_a.far_q = f32[11,1,64,128]{3,2,1,0:T(8,128)S(1)} collective-permute-done((f32[11,1,64,128]{3,2,1,0:T(8,128)S(1)}, f32[11,1,64,128]{3,2,1,0:T(8,128)S(1)}, u32[]{:S(2)}, u32[]{:S(2)}) %collective-permute-start.1) | collective-permute-done | bytes 360480 | tf_op jit(solution)/shard_map/ppermute | solution.py:373
  17.5 1.1 %first_0.1 = (f32[4,4,64,128]{3,2,1,0:T(8,128)S(1)}, f32[4,4,64,128]{3,2,1,0:T(8,128)S(1)}, f32[8,1,64,128]{3,2,1,0:T(8,128)S(1)}) custom-call(f32[4,4,64,128]{3,2,1,0:T(8,128)S(1)} %get-tuple-element.22.own, f32[12,5,64,128]{3,2,1,0:T(8,128)S(1)} %get-tuple-element.23.coefs, f32[11,1,64,128]{3,2,1,0:T(8,128)S(1)} %collective-permute-done.1.far_a.far_q, ...), custom_call_target="tpu_custom_call" | custom-call | flops 30000000 | bytes 6000000 | tf_op jit(solution)/shard_map/first_0/pallas_call | solution.py:437
  18.6 4.1 %collective-permute-start.2 = (f32[8,1,64,128]{3,2,1,0:T(8,128)S(1)}, f32[8,1,64,128]{3,2,1,0:T(8,128)S(1)}, u32[]{:S(2)}, u32[]{:S(2)}) collective-permute-start(f32[8,1,64,128]{3,2,1,0:T(8,128)S(1)} %get-tuple-element.32), channel_id=1, source_target_pairs={{0,32},{1,2},{2,1},{3,4},{4,3},{5,6},{6,5},{7,8},{8,7},{9,10},{10,... | collective-permute-start | bytes 786440 | tf_op jit(solution)/shard_map/ppermute | solution.py:373
  22.7 0.4 collective-permute-done.4.far_q
  23.1 1.1 %first_1.1 = (f32[4,4,64,128]{3,2,1,0:T(8,128)S(1)}, f32[4,4,64,128]{3,2,1,0:T(8,128)S(1)}, f32[8,1,64,128]{3,2,1,0:T(8,128)S(1)}) custom-call(f32[4,4,64,128]{3,2,1,0:T(8,128)S(1)} %get-tuple-element.28.own, f32[12,5,64,128]{3,2,1,0:T(8,128)S(1)} %get-tuple-element.23.coefs, f32[11,1,64,128]{3,2,1,0:T(8,128)S(1)} %collective-permute-done.1.far_a.far_q, ...), custom_call_target="tpu_custom_call" | custom-call | flops 30000000 | bytes 6000000 | tf_op jit(solution)/shard_map/first_1/pallas_call | solution.py:437
  24.2 4.1 %collective-permute-start.5 = (f32[8,1,64,128]{3,2,1,0:T(8,128)S(1)}, f32[8,1,64,128]{3,2,1,0:T(8,128)S(1)}, u32[]{:S(2)}, u32[]{:S(2)}) collective-permute-start(f32[8,1,64,128]{3,2,1,0:T(8,128)S(1)} %get-tuple-element.39), channel_id=1, source_target_pairs={{0,32},{1,2},{2,1},{3,4},{4,3},{5,6},{6,5},{7,8},{8,7},{9,10},{10,... | collective-permute-start | bytes 786440 | tf_op jit(solution)/shard_map/ppermute | solution.py:373
  28.3 2.6 %collective-permute-done.2.far_mid = f32[8,1,64,128]{3,2,1,0:T(8,128)S(1)} collective-permute-done((f32[8,1,64,128]{3,2,1,0:T(8,128)S(1)}, f32[8,1,64,128]{3,2,1,0:T(8,128)S(1)}, u32[]{:S(2)}, u32[]{:S(2)}) %collective-permute-start.2) | collective-permute-done | bytes 262176 | tf_op jit(solution)/shard_map/ppermute | solution.py:373
  30.9 2.0 %second_0.1.after.value = f32[4,4,64,128]{3,2,1,0:T(8,128)S(1)} custom-call(f32[4,4,64,128]{3,2,1,0:T(8,128)S(1)} %get-tuple-element.22.own, f32[12,5,64,128]{3,2,1,0:T(8,128)S(1)} %get-tuple-element.23.coefs, f32[11,2,64,128]{3,2,1,0:T(8,128)S(1)} %collective-permute-done.near, f32[11,1,64,128]{3,2,1,0:T(8,128)S(1)} %collective-permute-done.1.far_a.far_q, ...), custom_call_target="tpu_custom_call" | custom-call | flops 30000000 | bytes 6000000 | tf_op jit(solution)/shard_map/second_0/pallas_call | solution.py:448
  32.9 3.6 %collective-permute-done.5.far_mid.after = f32[8,1,64,128]{3,2,1,0:T(8,128)S(1)} collective-permute-done((f32[8,1,64,128]{3,2,1,0:T(8,128)S(1)}, f32[8,1,64,128]{3,2,1,0:T(8,128)S(1)}, u32[]{:S(2)}, u32[]{:S(2)}) %collective-permute-start.5) | collective-permute-done | bytes 262176 | tf_op jit(solution)/shard_map/ppermute | solution.py:373
  36.5 0.1 collective-permute-start.7
  36.6 2.0 %second_1.1 = f32[4,4,64,128]{3,2,1,0:T(8,128)S(1)} custom-call(f32[4,4,64,128]{3,2,1,0:T(8,128)S(1)} %get-tuple-element.28.own, f32[12,5,64,128]{3,2,1,0:T(8,128)S(1)} %get-tuple-element.23.coefs, f32[11,2,64,128]{3,2,1,0:T(8,128)S(1)} %collective-permute-done.near, f32[11,1,64,128]{3,2,1,0:T(8,128)S(1)} %collective-permute-done.1.far_a.far_q, ...), custom_call_target="tpu_custom_call" | custom-call | flops 30000000 | bytes 6000000 | tf_op jit(solution)/shard_map/second_1/pallas_call | solution.py:448
  38.6 2.9 %collective-permute-start.6 = (f32[4,4,64,128]{3,2,1,0:T(8,128)S(1)}, f32[4,4,64,128]{3,2,1,0:T(8,128)S(1)}, u32[]{:S(2)}, u32[]{:S(2)}) collective-permute-start(f32[4,4,64,128]{3,2,1,0:T(8,128)S(1)} %second_1.1), channel_id=1, source_target_pairs={{0,16},{16,32},{32,48},{48,64},{64,80},{80,96},{96,112},{112,0},{1... | collective-permute-start | bytes 1572872 | tf_op jit(solution)/shard_map/ppermute | solution.py:478
  41.5 1.1 %maximum_bitcast_fusion = f32[1,2,4,4,64,128]{5,4,3,2,1,0:T(8,128)} fusion(f32[1,4,4,64,128]{4,3,2,1,0:T(8,128)S(1)} %bitcast.5, f32[1,4,4,64,128]{4,3,2,1,0:T(8,128)S(1)} %bitcast.4), kind=kLoop, calls=%fused_computation | loop fusion | flops 262144 | bytes 2097152 | tf_op jit(solution)/shard_map/broadcast_in_dim | solution.py:479
  42.6 10.4 %collective-permute-done.7.previous = f32[4,4,64,128]{3,2,1,0:T(8,128)S(1)} collective-permute-done((f32[4,4,64,128]{3,2,1,0:T(8,128)S(1)}, f32[4,4,64,128]{3,2,1,0:T(8,128)S(1)}, u32[]{:S(2)}, u32[]{:S(2)}) %collective-permute-start.7) | collective-permute-done | bytes 524320 | tf_op jit(solution)/shard_map/ppermute | solution.py:476
  53.0 0.8 %residual_0.1.rest_0_ = f32[1,2,4,4,64,128]{5,4,3,2,1,0:T(8,128)} custom-call(f32[4,4,64,128]{3,2,1,0:T(8,128)S(1)} %get-tuple-element.22.own, f32[4,4,64,128]{3,2,1,0:T(8,128)S(1)} %collective-permute-done.7.previous), custom_call_target="tpu_custom_call" | custom-call | tf_op jit(solution)/shard_map/residual_0/pallas_call | solution.py:459
  53.8 4.6 %collective-permute-done.6.previous = f32[4,4,64,128]{3,2,1,0:T(8,128)S(1)} collective-permute-done((f32[4,4,64,128]{3,2,1,0:T(8,128)S(1)}, f32[4,4,64,128]{3,2,1,0:T(8,128)S(1)}, u32[]{:S(2)}, u32[]{:S(2)}) %collective-permute-start.6) | collective-permute-done | bytes 524320 | tf_op jit(solution)/shard_map/ppermute | solution.py:478
  58.4 0.8 %residual_1.1 = f32[1,2,4,4,64,128]{5,4,3,2,1,0:T(8,128)} custom-call(f32[4,4,64,128]{3,2,1,0:T(8,128)S(1)} %get-tuple-element.28.own, f32[4,4,64,128]{3,2,1,0:T(8,128)S(1)} %collective-permute-done.6.previous, f32[1,2,4,4,64,128]{5,4,3,2,1,0:T(8,128)} %residual_0.1.rest_0_), custom_call_target="tpu_custom_call", output_to_operand_aliasing={{}: (2, {})} | custom-call | tf_op jit(solution)/shard_map/residual_1/pallas_call | solution.py:459
  (3 shorter events, 0.1 us)
Async XLA Ops:
  2.0 4.5 %collective-permute-start = (f32[11,2,64,128]{3,2,1,0:T(8,128)S(1)}, f32[11,2,64,128]{3,2,1,0:T(8,128)S(1)}, u32[]{:S(2)}, u32[]{:S(2)}) collective-permute-start(f32[11,2,64,128]{3,2,1,0:T(8,128)S(1)} %get-tuple-element.21), channel_id=1, source_target_pairs={{0,1},{1,0},{2,3},{3,2},{4,5},{5,4},{6,7},{7,6},{8,9},{9,8},{10,11... | collective-permute-start | bytes 2162696 | tf_op jit(solution)/shard_map/ppermute | solution.py:376
  3.5 14.0 %collective-permute-start.1 = (f32[11,1,64,128]{3,2,1,0:T(8,128)S(1)}, f32[11,1,64,128]{3,2,1,0:T(8,128)S(1)}, u32[]{:S(2)}, u32[]{:S(2)}) collective-permute-start(f32[11,1,64,128]{3,2,1,0:T(8,128)S(1)} %get-tuple-element.24), channel_id=1, source_target_pairs={{0,32},{1,2},{2,1},{3,4},{4,3},{5,6},{6,5},{7,8},{8,7},{9,10},{10,... | collective-permute-start | bytes 1081352 | tf_op jit(solution)/shard_map/ppermute | solution.py:373
  10.4 12.7 %collective-permute-start.4 = (f32[8,1,64,128]{3,2,1,0:T(8,128)S(1)}, f32[8,1,64,128]{3,2,1,0:T(8,128)S(1)}, u32[]{:S(2)}, u32[]{:S(2)}) collective-permute-start(f32[8,1,64,128]{3,2,1,0:T(8,128)S(1)} %get-tuple-element.34), channel_id=1, source_target_pairs={{0,32},{1,2},{2,1},{3,4},{4,3},{5,6},{6,5},{7,8},{8,7},{9,10},{10,... | collective-permute-start | bytes 786440 | tf_op jit(solution)/shard_map/ppermute | solution.py:373
  12.6 18.3 %collective-permute-start.3 = (f32[8,2,64,128]{3,2,1,0:T(8,128)S(1)}, f32[8,2,64,128]{3,2,1,0:T(8,128)S(1)}, u32[]{:S(2)}, u32[]{:S(2)}) collective-permute-start(f32[8,2,64,128]{3,2,1,0:T(8,128)S(1)} %get-tuple-element.33), channel_id=1, source_target_pairs={{0,1},{1,0},{2,3},{3,2},{4,5},{5,4},{6,7},{7,6},{8,9},{9,8},{10,11... | collective-permute-start | bytes 1572872 | tf_op jit(solution)/shard_map/ppermute | solution.py:376
  18.6 12.3 %collective-permute-start.2 = (f32[8,1,64,128]{3,2,1,0:T(8,128)S(1)}, f32[8,1,64,128]{3,2,1,0:T(8,128)S(1)}, u32[]{:S(2)}, u32[]{:S(2)}) collective-permute-start(f32[8,1,64,128]{3,2,1,0:T(8,128)S(1)} %get-tuple-element.32), channel_id=1, source_target_pairs={{0,32},{1,2},{2,1},{3,4},{4,3},{5,6},{6,5},{7,8},{8,7},{9,10},{10,... | collective-permute-start | bytes 786440 | tf_op jit(solution)/shard_map/ppermute | solution.py:373
  24.2 12.3 %collective-permute-start.5 = (f32[8,1,64,128]{3,2,1,0:T(8,128)S(1)}, f32[8,1,64,128]{3,2,1,0:T(8,128)S(1)}, u32[]{:S(2)}, u32[]{:S(2)}) collective-permute-start(f32[8,1,64,128]{3,2,1,0:T(8,128)S(1)} %get-tuple-element.39), channel_id=1, source_target_pairs={{0,32},{1,2},{2,1},{3,4},{4,3},{5,6},{6,5},{7,8},{8,7},{9,10},{10,... | collective-permute-start | bytes 786440 | tf_op jit(solution)/shard_map/ppermute | solution.py:373
  36.5 16.4 %collective-permute-start.7 = (f32[4,4,64,128]{3,2,1,0:T(8,128)S(1)}, f32[4,4,64,128]{3,2,1,0:T(8,128)S(1)}, u32[]{:S(2)}, u32[]{:S(2)}) collective-permute-start(f32[4,4,64,128]{3,2,1,0:T(8,128)S(1)} %hold.1), channel_id=1, source_target_pairs={{0,16},{16,32},{32,48},{48,64},{64,80},{80,96},{96,112},{112,0},{1... | collective-permute-start | bytes 1572872 | tf_op jit(solution)/shard_map/ppermute | solution.py:476
  38.6 19.8 %collective-permute-start.6 = (f32[4,4,64,128]{3,2,1,0:T(8,128)S(1)}, f32[4,4,64,128]{3,2,1,0:T(8,128)S(1)}, u32[]{:S(2)}, u32[]{:S(2)}) collective-permute-start(f32[4,4,64,128]{3,2,1,0:T(8,128)S(1)} %second_1.1), channel_id=1, source_target_pairs={{0,16},{16,32},{32,48},{48,64},{64,80},{80,96},{96,112},{112,0},{1... | collective-permute-start | bytes 1572872 | tf_op jit(solution)/shard_map/ppermute | solution.py:478

commit v4 on v2

--- a/solution.py
+++ b/solution.py
@@ -348,9 +348,9 @@
 def residual_kernel(vec, own, previous, *rest):
     out, held, sems = rest[-3:]
     copies = []
-    for j in range(4):
-        held[j] = own[j] - previous[j]
-        copies.append(pltpu.make_async_copy(held.at[j], out.at[0, vec, j], sems.at[j]))
+    for j in range(2):
+        held[2 * j : 2 * j + 2] = own[2 * j : 2 * j + 2] - previous[2 * j : 2 * j + 2]
+        copies.append(pltpu.make_async_copy(held.at[2 * j : 2 * j + 2], out.at[0, vec, 2 * j : 2 * j + 2], sems.at[j]))
         copies[-1].start()
     for copy in copies:
         copy.wait()

time: 59.4 us -> 59.4 us (level)
  no operation moved by 1% of the time
where the time goes in v4:
time: 59.4 us; the launch traced here: 59.3 us
  waiting for transfers between devices  26.6 us (45%)
  starting transfers between devices  17.7 us (30%)
  Pallas kernels  13.2 us (22%)
  other arithmetic  1.08 us (2%)
  between operations  0.72 us (1%)
    ppermute x4, starting transfers between devices, far_swap(): return lax.ppermute(value, ('seg', 'slab'), far_pairs)  13.3 us
    ppermute x4, waiting for transfers between devices, far_swap(): return lax.ppermute(value, ('seg', 'slab'), far_pairs)  11.6 us
    ppermute x1, waiting for transfers between devices, shards(): prev0 = lax.ppermute(held0, 'seg', seg_pairs)  10.4 us
    ppermute x1, waiting for transfers between devices, shards(): prev1 = lax.ppermute(out1, 'seg', seg_pairs)  4.55 us
    pallas_call x2, Pallas kernels, second(): call(functools.partial(second_kernel, near_at, far_at), f'second_{vec}',...  3.97 us
    ppermute x1, starting transfers between devices, shards(): prev1 = lax.ppermute(out1, 'seg', seg_pairs)  2.86 us
    pallas_call x1, Pallas kernels, shards(): call(inner_0_kernel, 'inner_0', [anywhere] * 3, (planes(COEFS, COEF_PLANE...  2.68 us
    pallas_call x2, Pallas kernels, first(): call(functools.partial(first_kernel, far_at), f'first_{vec}', [anywhere,...  2.2 us
  transfers between devices with their start and end apart: 8, of which 6 were waited for; matrix products, arithmetic and copies ran while one was open for 2% of the time, Pallas kernels for 18%

profile of v4, /device:TPU:1, one launch (start us, length us, event | category | flops | bytes accessed | tf_op | source)
XLA Modules:
  0.0 59.3 jit_solution(5188587056246760988)
XLA Ops:
  0.6 1.4 %pack.1 = (f32[11,1,64,128]{3,2,1,0:T(8,128)S(1)}, f32[11,2,64,128]{3,2,1,0:T(8,128)S(1)}) custom-call(f32[1,2,4,4,64,128]{5,4,3,2,1,0:T(8,128)} %state.3, f32[1,3,4,64,128]{4,3,2,1,0:T(8,128)} %flow.3), custom_call_target="tpu_custom_call" | custom-call | tf_op jit(solution)/shard_map/pack/pallas_call | solution.py:405
  2.0 1.5 %collective-permute-start = (f32[11,2,64,128]{3,2,1,0:T(8,128)S(1)}, f32[11,2,64,128]{3,2,1,0:T(8,128)S(1)}, u32[]{:S(2)}, u32[]{:S(2)}) collective-permute-start(f32[11,2,64,128]{3,2,1,0:T(8,128)S(1)} %get-tuple-element.21), channel_id=1, source_target_pairs={{0,1},{1,0},{2,3},{3,2},{4,5},{5,4},{6,7},{7,6},{8,9},{9,8},{10,11... | collective-permute-start | bytes 2162696 | tf_op jit(solution)/shard_map/ppermute | solution.py:377
  3.5 3.0 %collective-permute-start.1 = (f32[11,1,64,128]{3,2,1,0:T(8,128)S(1)}, f32[11,1,64,128]{3,2,1,0:T(8,128)S(1)}, u32[]{:S(2)}, u32[]{:S(2)}) collective-permute-start(f32[11,1,64,128]{3,2,1,0:T(8,128)S(1)} %get-tuple-element.24), channel_id=1, source_target_pairs={{0,32},{1,2},{2,1},{3,4},{4,3},{5,6},{6,5},{7,8},{8,7},{9,10},{10,... | collective-permute-start | bytes 1081352 | tf_op jit(solution)/shard_map/ppermute | solution.py:374
  6.5 0.0 collective-permute-done.near
  6.5 2.7 %inner_0.1 = (f32[12,5,64,128]{3,2,1,0:T(8,128)S(1)}, f32[4,4,64,128]{3,2,1,0:T(8,128)S(1)}, f32[4,4,64,128]{3,2,1,0:T(8,128)S(1)}, f32[4,4,64,128]{3,2,1,0:T(8,...) custom-call(f32[1,2,4,4,64,128]{5,4,3,2,1,0:T(8,128)} %state.3, f32[1,3,4,64,128]{4,3,2,1,0:T(8,128)} %flow.3, ...), custom_call_target="tpu_custom_call" | custom-call | flops 30000000 | bytes 6000000 | tf_op jit(solution)/shard_map/inner_0/pallas_call | solution.py:416
  9.2 1.2 %inner_1.1 = (f32[4,4,64,128]{3,2,1,0:T(8,128)S(1)}, f32[4,2,64,128]{3,2,1,0:T(8,128)S(1)}, f32[4,2,64,128]{3,2,1,0:T(8,128)S(1)}, f32[8,1,64,128]{3,2,1,0:T(8,128)S(1)}, f32[8,2,64,128]{3,2,1,0:T(8,128)S(1)}) custom-call(f32[4,4,64,128]{3,2,1,0:T(8,128)S(1)} %get-tuple-element.28.own, f32[11,2,64,128]{3,2,1,0:T(8,128)S(1)} %collective-permute-done.near, ...), custom_call_target="tpu_custom_call" | custom-call | flops 30000000 | bytes 6000000 | tf_op jit(solution)/shard_map/inner_1/pallas_call | solution.py:425
  10.4 2.2 %collective-permute-start.4 = (f32[8,1,64,128]{3,2,1,0:T(8,128)S(1)}, f32[8,1,64,128]{3,2,1,0:T(8,128)S(1)}, u32[]{:S(2)}, u32[]{:S(2)}) collective-permute-start(f32[8,1,64,128]{3,2,1,0:T(8,128)S(1)} %get-tuple-element.34), channel_id=1, source_target_pairs={{0,32},{1,2},{2,1},{3,4},{4,3},{5,6},{6,5},{7,8},{8,7},{9,10},{10,... | collective-permute-start | bytes 786440 | tf_op jit(solution)/shard_map/ppermute | solution.py:374
  12.6 5.0 %collective-permute-done.1.far_a.far_q = f32[11,1,64,128]{3,2,1,0:T(8,128)S(1)} collective-permute-done((f32[11,1,64,128]{3,2,1,0:T(8,128)S(1)}, f32[11,1,64,128]{3,2,1,0:T(8,128)S(1)}, u32[]{:S(2)}, u32[]{:S(2)}) %collective-permute-start.1) | collective-permute-done | bytes 360480 | tf_op jit(solution)/shard_map/ppermute | solution.py:374
  17.5 1.1 %first_0.1 = (f32[4,4,64,128]{3,2,1,0:T(8,128)S(1)}, f32[4,4,64,128]{3,2,1,0:T(8,128)S(1)}, f32[8,1,64,128]{3,2,1,0:T(8,128)S(1)}) custom-call(f32[4,4,64,128]{3,2,1,0:T(8,128)S(1)} %get-tuple-element.22.own, f32[12,5,64,128]{3,2,1,0:T(8,128)S(1)} %get-tuple-element.23.coefs, f32[11,1,64,128]{3,2,1,0:T(8,128)S(1)} %collective-permute-done.1.far_a.far_q, ...), custom_call_target="tpu_custom_call" | custom-call | flops 30000000 | bytes 6000000 | tf_op jit(solution)/shard_map/first_0/pallas_call | solution.py:438
  18.6 4.1 %collective-permute-start.2 = (f32[8,1,64,128]{3,2,1,0:T(8,128)S(1)}, f32[8,1,64,128]{3,2,1,0:T(8,128)S(1)}, u32[]{:S(2)}, u32[]{:S(2)}) collective-permute-start(f32[8,1,64,128]{3,2,1,0:T(8,128)S(1)} %get-tuple-element.32), channel_id=1, source_target_pairs={{0,32},{1,2},{2,1},{3,4},{4,3},{5,6},{6,5},{7,8},{8,7},{9,10},{10,... | collective-permute-start | bytes 786440 | tf_op jit(solution)/shard_map/ppermute | solution.py:374
  22.7 0.4 collective-permute-done.4.far_q
  23.1 1.1 %first_1.1 = (f32[4,4,64,128]{3,2,1,0:T(8,128)S(1)}, f32[4,4,64,128]{3,2,1,0:T(8,128)S(1)}, f32[8,1,64,128]{3,2,1,0:T(8,128)S(1)}) custom-call(f32[4,4,64,128]{3,2,1,0:T(8,128)S(1)} %get-tuple-element.28.own, f32[12,5,64,128]{3,2,1,0:T(8,128)S(1)} %get-tuple-element.23.coefs, f32[11,1,64,128]{3,2,1,0:T(8,128)S(1)} %collective-permute-done.1.far_a.far_q, ...), custom_call_target="tpu_custom_call" | custom-call | flops 30000000 | bytes 6000000 | tf_op jit(solution)/shard_map/first_1/pallas_call | solution.py:438
  24.2 4.1 %collective-permute-start.5 = (f32[8,1,64,128]{3,2,1,0:T(8,128)S(1)}, f32[8,1,64,128]{3,2,1,0:T(8,128)S(1)}, u32[]{:S(2)}, u32[]{:S(2)}) collective-permute-start(f32[8,1,64,128]{3,2,1,0:T(8,128)S(1)} %get-tuple-element.39), channel_id=1, source_target_pairs={{0,32},{1,2},{2,1},{3,4},{4,3},{5,6},{6,5},{7,8},{8,7},{9,10},{10,... | collective-permute-start | bytes 786440 | tf_op jit(solution)/shard_map/ppermute | solution.py:374
  28.3 2.6 %collective-permute-done.2.far_mid = f32[8,1,64,128]{3,2,1,0:T(8,128)S(1)} collective-permute-done((f32[8,1,64,128]{3,2,1,0:T(8,128)S(1)}, f32[8,1,64,128]{3,2,1,0:T(8,128)S(1)}, u32[]{:S(2)}, u32[]{:S(2)}) %collective-permute-start.2) | collective-permute-done | bytes 262176 | tf_op jit(solution)/shard_map/ppermute | solution.py:374
  30.9 2.0 %second_0.1.after.value = f32[4,4,64,128]{3,2,1,0:T(8,128)S(1)} custom-call(f32[4,4,64,128]{3,2,1,0:T(8,128)S(1)} %get-tuple-element.22.own, f32[12,5,64,128]{3,2,1,0:T(8,128)S(1)} %get-tuple-element.23.coefs, f32[11,2,64,128]{3,2,1,0:T(8,128)S(1)} %collective-permute-done.near, f32[11,1,64,128]{3,2,1,0:T(8,128)S(1)} %collective-permute-done.1.far_a.far_q, ...), custom_call_target="tpu_custom_call" | custom-call | flops 30000000 | bytes 6000000 | tf_op jit(solution)/shard_map/second_0/pallas_call | solution.py:449
  32.9 3.6 %collective-permute-done.5.far_mid.after = f32[8,1,64,128]{3,2,1,0:T(8,128)S(1)} collective-permute-done((f32[8,1,64,128]{3,2,1,0:T(8,128)S(1)}, f32[8,1,64,128]{3,2,1,0:T(8,128)S(1)}, u32[]{:S(2)}, u32[]{:S(2)}) %collective-permute-start.5) | collective-permute-done | bytes 262176 | tf_op jit(solution)/shard_map/ppermute | solution.py:374
  36.6 0.1 collective-permute-start.7
  36.6 2.0 %second_1.1 = f32[4,4,64,128]{3,2,1,0:T(8,128)S(1)} custom-call(f32[4,4,64,128]{3,2,1,0:T(8,128)S(1)} %get-tuple-element.28.own, f32[12,5,64,128]{3,2,1,0:T(8,128)S(1)} %get-tuple-element.23.coefs, f32[11,2,64,128]{3,2,1,0:T(8,128)S(1)} %collective-permute-done.near, f32[11,1,64,128]{3,2,1,0:T(8,128)S(1)} %collective-permute-done.1.far_a.far_q, ...), custom_call_target="tpu_custom_call" | custom-call | flops 30000000 | bytes 6000000 | tf_op jit(solution)/shard_map/second_1/pallas_call | solution.py:449
  38.6 2.9 %collective-permute-start.6 = (f32[4,4,64,128]{3,2,1,0:T(8,128)S(1)}, f32[4,4,64,128]{3,2,1,0:T(8,128)S(1)}, u32[]{:S(2)}, u32[]{:S(2)}) collective-permute-start(f32[4,4,64,128]{3,2,1,0:T(8,128)S(1)} %second_1.1), channel_id=1, source_target_pairs={{0,16},{16,32},{32,48},{48,64},{64,80},{80,96},{96,112},{112,0},{1... | collective-permute-start | bytes 1572872 | tf_op jit(solution)/shard_map/ppermute | solution.py:479
  41.5 1.1 %maximum_bitcast_fusion = f32[1,2,4,4,64,128]{5,4,3,2,1,0:T(8,128)} fusion(f32[1,4,4,64,128]{4,3,2,1,0:T(8,128)S(1)} %bitcast.5, f32[1,4,4,64,128]{4,3,2,1,0:T(8,128)S(1)} %bitcast.4), kind=kLoop, calls=%fused_computation | loop fusion | flops 262144 | bytes 2097152 | tf_op jit(solution)/shard_map/broadcast_in_dim | solution.py:480
  42.6 10.4 %collective-permute-done.7.previous = f32[4,4,64,128]{3,2,1,0:T(8,128)S(1)} collective-permute-done((f32[4,4,64,128]{3,2,1,0:T(8,128)S(1)}, f32[4,4,64,128]{3,2,1,0:T(8,128)S(1)}, u32[]{:S(2)}, u32[]{:S(2)}) %collective-permute-start.7) | collective-permute-done | bytes 524320 | tf_op jit(solution)/shard_map/ppermute | solution.py:477
  53.0 0.9 %residual_0.1.rest_0_ = f32[1,2,4,4,64,128]{5,4,3,2,1,0:T(8,128)} custom-call(f32[4,4,64,128]{3,2,1,0:T(8,128)S(1)} %get-tuple-element.22.own, f32[4,4,64,128]{3,2,1,0:T(8,128)S(1)} %collective-permute-done.7.previous), custom_call_target="tpu_custom_call" | custom-call | tf_op jit(solution)/shard_map/residual_0/pallas_call | solution.py:460
  53.9 4.6 %collective-permute-done.6.previous = f32[4,4,64,128]{3,2,1,0:T(8,128)S(1)} collective-permute-done((f32[4,4,64,128]{3,2,1,0:T(8,128)S(1)}, f32[4,4,64,128]{3,2,1,0:T(8,128)S(1)}, u32[]{:S(2)}, u32[]{:S(2)}) %collective-permute-start.6) | collective-permute-done | bytes 524320 | tf_op jit(solution)/shard_map/ppermute | solution.py:479
  58.4 0.9 %residual_1.1 = f32[1,2,4,4,64,128]{5,4,3,2,1,0:T(8,128)} custom-call(f32[4,4,64,128]{3,2,1,0:T(8,128)S(1)} %get-tuple-element.28.own, f32[4,4,64,128]{3,2,1,0:T(8,128)S(1)} %collective-permute-done.6.previous, f32[1,2,4,4,64,128]{5,4,3,2,1,0:T(8,128)} %residual_0.1.rest_0_), custom_call_target="tpu_custom_call", output_to_operand_aliasing={{}: (2, {})} | custom-call | tf_op jit(solution)/shard_map/residual_1/pallas_call | solution.py:460
  (3 shorter events, 0.1 us)
Async XLA Ops:
  2.0 4.5 %collective-permute-start = (f32[11,2,64,128]{3,2,1,0:T(8,128)S(1)}, f32[11,2,64,128]{3,2,1,0:T(8,128)S(1)}, u32[]{:S(2)}, u32[]{:S(2)}) collective-permute-start(f32[11,2,64,128]{3,2,1,0:T(8,128)S(1)} %get-tuple-element.21), channel_id=1, source_target_pairs={{0,1},{1,0},{2,3},{3,2},{4,5},{5,4},{6,7},{7,6},{8,9},{9,8},{10,11... | collective-permute-start | bytes 2162696 | tf_op jit(solution)/shard_map/ppermute | solution.py:377
  3.5 14.0 %collective-permute-start.1 = (f32[11,1,64,128]{3,2,1,0:T(8,128)S(1)}, f32[11,1,64,128]{3,2,1,0:T(8,128)S(1)}, u32[]{:S(2)}, u32[]{:S(2)}) collective-permute-start(f32[11,1,64,128]{3,2,1,0:T(8,128)S(1)} %get-tuple-element.24), channel_id=1, source_target_pairs={{0,32},{1,2},{2,1},{3,4},{4,3},{5,6},{6,5},{7,8},{8,7},{9,10},{10,... | collective-permute-start | bytes 1081352 | tf_op jit(solution)/shard_map/ppermute | solution.py:374
  10.4 12.7 %collective-permute-start.4 = (f32[8,1,64,128]{3,2,1,0:T(8,128)S(1)}, f32[8,1,64,128]{3,2,1,0:T(8,128)S(1)}, u32[]{:S(2)}, u32[]{:S(2)}) collective-permute-start(f32[8,1,64,128]{3,2,1,0:T(8,128)S(1)} %get-tuple-element.34), channel_id=1, source_target_pairs={{0,32},{1,2},{2,1},{3,4},{4,3},{5,6},{6,5},{7,8},{8,7},{9,10},{10,... | collective-permute-start | bytes 786440 | tf_op jit(solution)/shard_map/ppermute | solution.py:374
  12.6 18.3 %collective-permute-start.3 = (f32[8,2,64,128]{3,2,1,0:T(8,128)S(1)}, f32[8,2,64,128]{3,2,1,0:T(8,128)S(1)}, u32[]{:S(2)}, u32[]{:S(2)}) collective-permute-start(f32[8,2,64,128]{3,2,1,0:T(8,128)S(1)} %get-tuple-element.33), channel_id=1, source_target_pairs={{0,1},{1,0},{2,3},{3,2},{4,5},{5,4},{6,7},{7,6},{8,9},{9,8},{10,11... | collective-permute-start | bytes 1572872 | tf_op jit(solution)/shard_map/ppermute | solution.py:377
  18.6 12.3 %collective-permute-start.2 = (f32[8,1,64,128]{3,2,1,0:T(8,128)S(1)}, f32[8,1,64,128]{3,2,1,0:T(8,128)S(1)}, u32[]{:S(2)}, u32[]{:S(2)}) collective-permute-start(f32[8,1,64,128]{3,2,1,0:T(8,128)S(1)} %get-tuple-element.32), channel_id=1, source_target_pairs={{0,32},{1,2},{2,1},{3,4},{4,3},{5,6},{6,5},{7,8},{8,7},{9,10},{10,... | collective-permute-start | bytes 786440 | tf_op jit(solution)/shard_map/ppermute | solution.py:374
  24.2 12.3 %collective-permute-start.5 = (f32[8,1,64,128]{3,2,1,0:T(8,128)S(1)}, f32[8,1,64,128]{3,2,1,0:T(8,128)S(1)}, u32[]{:S(2)}, u32[]{:S(2)}) collective-permute-start(f32[8,1,64,128]{3,2,1,0:T(8,128)S(1)} %get-tuple-element.39), channel_id=1, source_target_pairs={{0,32},{1,2},{2,1},{3,4},{4,3},{5,6},{6,5},{7,8},{8,7},{9,10},{10,... | collective-permute-start | bytes 786440 | tf_op jit(solution)/shard_map/ppermute | solution.py:374
  36.6 16.4 %collective-permute-start.7 = (f32[4,4,64,128]{3,2,1,0:T(8,128)S(1)}, f32[4,4,64,128]{3,2,1,0:T(8,128)S(1)}, u32[]{:S(2)}, u32[]{:S(2)}) collective-permute-start(f32[4,4,64,128]{3,2,1,0:T(8,128)S(1)} %hold.1), channel_id=1, source_target_pairs={{0,16},{16,32},{32,48},{48,64},{64,80},{80,96},{96,112},{112,0},{1... | collective-permute-start | bytes 1572872 | tf_op jit(solution)/shard_map/ppermute | solution.py:477
  38.6 19.8 %collective-permute-start.6 = (f32[4,4,64,128]{3,2,1,0:T(8,128)S(1)}, f32[4,4,64,128]{3,2,1,0:T(8,128)S(1)}, u32[]{:S(2)}, u32[]{:S(2)}) collective-permute-start(f32[4,4,64,128]{3,2,1,0:T(8,128)S(1)} %second_1.1), channel_id=1, source_target_pairs={{0,16},{16,32},{32,48},{48,64},{64,80},{80,96},{96,112},{112,0},{1... | collective-permute-start | bytes 1572872 | tf_op jit(solution)/shard_map/ppermute | solution.py:479
